TPU v7x, 512 devices: a whole 4x8x8 slice. The times are simulated.
512 devices in a mesh: dp: 32 (over z, x_lo, core), dap: 16 (over y, x_hi).
Axes of the slice: x: 4 (x_hi: 2, x_lo: 2; x = x_hi * 2 + x_lo), y: 8, z: 8, core: 2. Of those that a mesh axis runs over, the one named last changes fastest.
Arguments:
- pair_repr: bfloat16 [32, 128, 128, 128], P('dp', 'dap'), may hold values from -6 to 6
- cotangent: bfloat16 [32, 128, 128, 128], P('dp', None, 'dap'), may hold values from -6 to 6
- residue_mask: int32 [32, 128], P('dp'), may hold values 0 or 1
- norm_gains: float32 [3, 128], replicated, may hold values from 0.1 to 1.9
- w_proj: bfloat16 [4, 128, 128], replicated, may hold values from -0.5 to 0.5
- w_out: bfloat16 [2, 128, 128], replicated, may hold values from -0.5 to 0.5
- w_up: bfloat16 [128, 512], replicated, may hold values from -0.5 to 0.5
- w_down: bfloat16 [512, 128], replicated, may hold values from -0.25 to 0.25
Outputs:
- pair_next: bfloat16 [32, 128, 128, 128], P('dp', None, 'dap')
- pair_grad: bfloat16 [32, 128, 128, 128], P('dp', 'dap')
- grad_proj: bfloat16 [4, 128, 128], replicated
- grad_out: bfloat16 [2, 128, 128], replicated
- grad_up: bfloat16 [128, 512], replicated
- grad_down: bfloat16 [512, 128], replicated
- grad_gains: bfloat16 [3, 128], replicated
Inputs may be any that keep to these rules, and one draw needn't show every extreme that they name: `residue_mask`: 1 marks a residue inside the crop, 0 padding.
All inputs are finite; a program needn't handle non-finite values. No bound on the sum of `residue_mask` on one device may be relied on, other than what follows from the above.
Results may differ from a plain program's by a relative error of at most 0.022.
Values may be sent and summed in bfloat16 or wider, within the bound.
A program may use at most 64 MiB of HBM per device.

v0:
```python
import math

import jax
import jax.numpy as jnp
from jax import lax
from jax.sharding import PartitionSpec as P

EPSILON = 1e-05
GELU_SCALE = 0.7978845608028654
GELU_CUBIC = 0.044715


def normalize(values, gain_row):
    average = jnp.mean(values, axis=-1, keepdims=True)
    centred = values - average
    inv_std = lax.rsqrt(jnp.mean(centred * centred, axis=-1, keepdims=True) + EPSILON)
    normed = centred * inv_std
    return (normed * gain_row, normed, inv_std)


def normalize_back(incoming, normed, inv_std, gain_row):
    scaled = incoming * gain_row
    inner_sum = (
        scaled
        - jnp.mean(scaled, axis=-1, keepdims=True)
        - normed * jnp.mean(scaled * normed, axis=-1, keepdims=True)
    )
    return (inv_std * inner_sum, jnp.sum(incoming * normed, axis=0))


def gelu_parts(pre_act):
    tanh_value = jnp.tanh(GELU_SCALE * (pre_act + GELU_CUBIC * pre_act * pre_act * pre_act))
    activation = 0.5 * pre_act * (1.0 + tanh_value)
    slopes = 0.5 * (1.0 + tanh_value) + 0.5 * pre_act * (
        1.0 - tanh_value * tanh_value
    ) * GELU_SCALE * (1.0 + 3.0 * GELU_CUBIC * pre_act * pre_act)
    return (activation, slopes)


def matmul(left_side, right_side):
    return jnp.dot(left_side, right_side, preferred_element_type=jnp.float32)


def weight_grad(inputs, outputs):
    return lax.dot_general(
        inputs, outputs, (((0,), (0,)), ((), ())), preferred_element_type=jnp.float32
    )


def front_pass(pair_rows, pair_mask, gain_rows, w_proj):
    pair_f = pair_rows.astype(jnp.float32)
    normed_out, pair_hat, pair_rstd = normalize(pair_f, gain_rows[0])
    pair_ln = normed_out.astype(jnp.bfloat16)
    a_gate = jax.nn.sigmoid(matmul(pair_ln, w_proj[0]))
    a_value = matmul(pair_ln, w_proj[1])
    b_gate = jax.nn.sigmoid(matmul(pair_ln, w_proj[2]))
    b_value = matmul(pair_ln, w_proj[3])
    left_proj = (pair_mask * a_gate * a_value).astype(jnp.bfloat16)
    right_proj = (pair_mask * b_gate * b_value).astype(jnp.bfloat16)
    stored = (pair_f, pair_ln, pair_hat, pair_rstd, a_gate, a_value, b_gate, b_value)
    return (left_proj, right_proj, stored)


def middle_pass(tri_sum, stored_front, gain_rows, w_out, w_up, w_down):
    pair_f = stored_front[0]
    pair_ln = stored_front[1]
    normed_out, tri_hat, tri_rstd = normalize(tri_sum, gain_rows[1])
    tri_ln = normed_out.astype(jnp.bfloat16)
    out_gate = jax.nn.sigmoid(matmul(pair_ln, w_out[0]))
    out_value = matmul(tri_ln, w_out[1])
    pair_mid = (pair_f + out_gate * out_value).astype(jnp.bfloat16)
    mid_f = pair_mid.astype(jnp.float32)
    normed_mid, mid_hat, mid_rstd = normalize(mid_f, gain_rows[2])
    mid_ln = normed_mid.astype(jnp.bfloat16)
    activation, slopes = gelu_parts(matmul(mid_ln, w_up))
    hidden = activation.astype(jnp.bfloat16)
    pair_out = (mid_f + matmul(hidden, w_down)).astype(jnp.bfloat16)
    stored = (
        tri_ln,
        tri_hat,
        tri_rstd,
        out_gate,
        out_value,
        mid_ln,
        mid_hat,
        mid_rstd,
        slopes,
        hidden,
    )
    return (pair_out, stored)


def upper_back(cot_rows, stored_front, stored_mid, gain_rows, w_out, w_up, w_down):
    tri_ln, tri_hat, tri_rstd, out_gate, out_value, mid_ln, mid_hat, mid_rstd, slopes, hidden = (
        stored_mid
    )
    pair_ln = stored_front[1]
    grad_down = weight_grad(hidden, cot_rows)
    d_pre = (matmul(cot_rows, w_down.T) * slopes).astype(jnp.bfloat16)
    grad_up = weight_grad(mid_ln, d_pre)
    d_norm, gain_mid = normalize_back(matmul(d_pre, w_up.T), mid_hat, mid_rstd, gain_rows[2])
    d_mid = d_norm + cot_rows.astype(jnp.float32)
    d_gate = (d_mid * out_value * out_gate * (1.0 - out_gate)).astype(jnp.bfloat16)
    d_value = (d_mid * out_gate).astype(jnp.bfloat16)
    grad_gate = weight_grad(pair_ln, d_gate)
    grad_value = weight_grad(tri_ln, d_value)
    d_tri, gain_tri = normalize_back(matmul(d_value, w_out[1].T), tri_hat, tri_rstd, gain_rows[1])
    return (
        d_tri.astype(jnp.bfloat16),
        d_mid,
        d_gate,
        (grad_down, grad_up, gain_mid),
        (grad_gate, grad_value, gain_tri),
    )


def lower_back(d_left, d_right, d_mid, d_gate, stored_front, pair_mask, gain_rows, w_proj, w_out):
    pair_ln = stored_front[1]
    pair_hat = stored_front[2]
    pair_rstd = stored_front[3]
    a_gate, a_value, b_gate, b_value = (
        stored_front[4],
        stored_front[5],
        stored_front[6],
        stored_front[7],
    )
    left_masked = d_left * pair_mask
    right_masked = d_right * pair_mask
    d_ag = (left_masked * a_value * a_gate * (1.0 - a_gate)).astype(jnp.bfloat16)
    d_av = (left_masked * a_gate).astype(jnp.bfloat16)
    d_bg = (right_masked * b_value * b_gate * (1.0 - b_gate)).astype(jnp.bfloat16)
    d_bv = (right_masked * b_gate).astype(jnp.bfloat16)
    grad_proj = jnp.stack(
        [
            weight_grad(pair_ln, d_ag),
            weight_grad(pair_ln, d_av),
            weight_grad(pair_ln, d_bg),
            weight_grad(pair_ln, d_bv),
        ]
    )
    d_ln = (
        matmul(d_gate, w_out[0].T)
        + matmul(d_ag, w_proj[0].T)
        + matmul(d_av, w_proj[1].T)
        + matmul(d_bg, w_proj[2].T)
        + matmul(d_bv, w_proj[3].T)
    )
    d_pair, gain_pair = normalize_back(d_ln, pair_hat, pair_rstd, gain_rows[0])
    return ((d_mid + d_pair).astype(jnp.bfloat16), grad_proj, gain_pair)


def local(pair_repr, cotangent, residue_mask, norm_gains, w_proj, w_out, w_up, w_down):
    own_rows = pair_repr.shape[1]
    residues = pair_repr.shape[2]
    channels = pair_repr.shape[3]
    row_count = own_rows * residues
    first_row = lax.axis_index("dap") * own_rows
    mask_f = residue_mask[0].astype(jnp.float32)
    mask_rows = lax.dynamic_slice_in_dim(mask_f, first_row, own_rows, 0)
    pair_mask = (mask_rows[:, None] * mask_f[None, :]).reshape(row_count, 1)
    left_proj, right_proj, stored_front = front_pass(
        pair_repr[0].reshape(row_count, channels), pair_mask, norm_gains, w_proj
    )
    left_chan = left_proj.reshape(own_rows, residues, channels).transpose(2, 0, 1)
    right_chan = right_proj.reshape(own_rows, residues, channels).transpose(2, 0, 1)
    left_cols, right_cols = (
        lax.all_to_all(left_chan, "dap", split_axis=0, concat_axis=1, tiled=True),
        lax.all_to_all(right_chan, "dap", split_axis=0, concat_axis=1, tiled=True),
    )
    tri_part_chan = jnp.einsum(
        "cik,cjk->cij", left_cols, right_cols, preferred_element_type=jnp.float32
    )
    tri_back = lax.all_to_all(
        tri_part_chan.astype(jnp.bfloat16), "dap", split_axis=1, concat_axis=0, tiled=True
    ).astype(tri_part_chan.dtype)
    tri_cube = tri_back.transpose(1, 2, 0)
    pair_out, stored_mid = middle_pass(
        tri_cube.reshape(row_count, channels), stored_front, norm_gains, w_out, w_up, w_down
    )
    pair_next = lax.all_to_all(
        pair_out.reshape(own_rows, residues, channels),
        "dap",
        split_axis=1,
        concat_axis=0,
        tiled=True,
    )
    cot_rows = lax.all_to_all(cotangent[0], "dap", split_axis=0, concat_axis=1, tiled=True)
    d_tri, d_mid, d_gate, trans_part, tri_part = upper_back(
        cot_rows.reshape(row_count, channels),
        stored_front,
        stored_mid,
        norm_gains,
        w_out,
        w_up,
        w_down,
    )
    grad_scale = 1.0 / math.sqrt(
        lax.axis_size("dp") * pair_repr.shape[0] * lax.axis_size("dap") * row_count
    )
    down_term = trans_part[0] * grad_scale
    up_term = trans_part[1] * grad_scale
    mid_gain_term = trans_part[2] * grad_scale
    d_chan = d_tri.reshape(own_rows, residues, channels).transpose(2, 0, 1)
    d_cols, left_again, right_again = (
        lax.all_to_all(d_chan, "dap", split_axis=0, concat_axis=1, tiled=True),
        lax.all_to_all(left_chan, "dap", split_axis=0, concat_axis=1, tiled=True),
        lax.all_to_all(right_chan, "dap", split_axis=0, concat_axis=1, tiled=True),
    )
    d_left_chan = jnp.einsum(
        "cij,cjk->cik", d_cols, right_again, preferred_element_type=jnp.float32
    )
    d_right_chan = jnp.einsum(
        "cij,cik->cjk", d_cols, left_again, preferred_element_type=jnp.float32
    )
    d_left_back, d_right_back = (
        lax.all_to_all(
            d_left_chan.astype(jnp.bfloat16), "dap", split_axis=1, concat_axis=0, tiled=True
        ).astype(d_left_chan.dtype),
        lax.all_to_all(
            d_right_chan.astype(jnp.bfloat16), "dap", split_axis=1, concat_axis=0, tiled=True
        ).astype(d_right_chan.dtype),
    )
    d_left = d_left_back.transpose(1, 2, 0).reshape(row_count, channels)
    d_right = d_right_back.transpose(1, 2, 0).reshape(row_count, channels)
    pair_grad, grad_proj, gain_pair = lower_back(
        d_left, d_right, d_mid, d_gate, stored_front, pair_mask, norm_gains, w_proj, w_out
    )
    proj_term = grad_proj * grad_scale
    out_term = jnp.stack([tri_part[0], tri_part[1]]) * grad_scale
    pair_gain_term = gain_pair * grad_scale
    tri_gain_term = tri_part[2] * grad_scale
    down_sum, up_sum, mid_gain_sum, proj_sum, out_sum, pair_gain_sum, tri_gain_sum = lax.psum(
        (down_term, up_term, mid_gain_term, proj_term, out_term, pair_gain_term, tri_gain_term),
        ("dp", "dap"),
    )
    grad_gains = jnp.stack([pair_gain_sum, tri_gain_sum, mid_gain_sum]).astype(jnp.bfloat16)
    return (
        pair_next[None],
        pair_grad.reshape(own_rows, residues, channels)[None],
        proj_sum.astype(jnp.bfloat16),
        out_sum.astype(jnp.bfloat16),
        up_sum.astype(jnp.bfloat16),
        down_sum.astype(jnp.bfloat16),
        grad_gains,
    )


def solution(mesh):
    in_specs = (
        P("dp", "dap", None, None),
        P("dp", None, "dap", None),
        P("dp", None),
        P(),
        P(),
        P(),
        P(),
        P(),
    )
    out_specs = (P("dp", None, "dap", None), P("dp", "dap", None, None), P(), P(), P(), P(), P())
    return jax.shard_map(local, mesh=mesh, in_specs=in_specs, out_specs=out_specs, check_vma=False)
```

profile of v0, /device:TPU:1, one launch (start us, length us, event | category | flops | bytes accessed | tf_op | source)
XLA Modules:
  0.0 272.1 jit_solution(9629163502498489827)
XLA Ops:
  2.6 1.3 fusion.33
  4.0 1.3 fusion.35
  9.7 10.2 %all-to-all-start.1 = ((bf16[128,8,128]{2,1,0:T(8,128)(2,1)}), bf16[128,8,128]{2,1,0:T(8,128)(2,1)S(1)}, u32[]{:S(2)}, u32[]{:S(2)}) async-start(bf16[128,8,128]{2,1,0:T(8,128)(2,1)} %bitcast.17), calls=%async_computation.1 | async-start | bytes 524288 | tf_op jit(solution)/shard_map/all_to_all | solution.py:168
  20.2 11.8 %all-to-all-done.1 = bf16[128,8,128]{2,1,0:T(8,128)(2,1)S(1)} async-done(((bf16[128,8,128]{2,1,0:T(8,128)(2,1)}), bf16[128,8,128]{2,1,0:T(8,128)(2,1)S(1)}, u32[]{:S(2)}, u32[]{:S(2)}) %all-to-all-start.1) | async-done | bytes 262176 | tf_op jit(solution)/shard_map/all_to_all | solution.py:168
  31.9 14.4 %all_to_all.121 = bf16[128,8,128]{2,1,0:T(8,128)(2,1)S(1)} all-to-all(bf16[128,8,128]{2,1,0:T(8,128)(2,1)S(1)} %bitcast.264), channel_id=1, replica_groups=mesh['dp'=32,'dap'=16] {'dap'}, dimensions={0} | all-to-all | bytes 524288 | tf_op jit(solution)/shard_map/all_to_all | solution.py:167
  46.3 3.5 %all-to-all-start.4 = ((bf16[128,8,128]{2,1,0:T(8,128)(2,1)}), bf16[128,8,128]{2,1,0:T(8,128)(2,1)S(1)}, u32[]{:S(2)}, u32[]{:S(2)}) async-start(bf16[128,8,128]{2,1,0:T(8,128)(2,1)} %bitcast.33), calls=%async_computation.4 | async-start | bytes 524288 | tf_op jit(solution)/shard_map/all_to_all | solution.py:187
  51.1 10.0 %all-to-all-done.4 = bf16[128,8,128]{2,1,0:T(8,128)(2,1)S(1)} async-done(((bf16[128,8,128]{2,1,0:T(8,128)(2,1)}), bf16[128,8,128]{2,1,0:T(8,128)(2,1)S(1)}, u32[]{:S(2)}, u32[]{:S(2)}) %all-to-all-start.4) | async-done | bytes 262176 | tf_op jit(solution)/shard_map/all_to_all | solution.py:187
  61.0 3.5 %all-to-all-start.2 = ((bf16[8,128,128]{2,0,1:T(8,128)(2,1)}), bf16[8,128,128]{2,0,1:T(8,128)(2,1)S(1)}, u32[]{:S(2)}, u32[]{:S(2)}) async-start(bf16[8,128,128]{2,0,1:T(8,128)(2,1)} %copy.58), calls=%async_computation.2 | async-start | bytes 524288 | tf_op jit(solution)/shard_map/all_to_all | solution.py:173
  64.6 11.0 %all-to-all-done.2 = bf16[8,128,128]{2,0,1:T(8,128)(2,1)S(1)} async-done(((bf16[8,128,128]{2,0,1:T(8,128)(2,1)}), bf16[8,128,128]{2,0,1:T(8,128)(2,1)S(1)}, u32[]{:S(2)}, u32[]{:S(2)}) %all-to-all-start.2) | async-done | bytes 262176 | tf_op jit(solution)/shard_map/all_to_all | solution.py:173
  79.7 1.4 fusion.6
  82.2 2.2 multiply_convert_fusion.7
  84.4 1.6 multiply_reduce_fusion
  86.0 1.3 multiply_convert_fusion.6
  87.4 1.8 copy.65
  89.2 3.5 %all-to-all-start.5 = ((bf16[128,8,128]{2,1,0:T(8,128)(2,1)}), bf16[128,8,128]{2,1,0:T(8,128)(2,1)S(1)}, u32[]{:S(2)}, u32[]{:S(2)}) async-start(bf16[128,8,128]{2,1,0:T(8,128)(2,1)} %bitcast.43), calls=%async_computation.5 | async-start | bytes 524288 | tf_op jit(solution)/shard_map/all_to_all | solution.py:205
  92.8 1.4 fusion.16
  95.0 1.2 broadcast_multiply_fusion.9
  96.2 1.2 broadcast_multiply_fusion.10
  97.4 6.4 %all-to-all-done.5 = bf16[128,8,128]{2,1,0:T(8,128)(2,1)S(1)} async-done(((bf16[128,8,128]{2,1,0:T(8,128)(2,1)}), bf16[128,8,128]{2,1,0:T(8,128)(2,1)S(1)}, u32[]{:S(2)}, u32[]{:S(2)}) %all-to-all-start.5) | async-done | bytes 262176 | tf_op jit(solution)/shard_map/all_to_all | solution.py:205
  103.8 4.2 %all-to-all-start.3 = ((bf16[8,128,128]{2,0,1:T(8,128)(2,1)}), bf16[8,128,128]{2,0,1:T(8,128)(2,1)}, u32[]{:S(2)}, u32[]{:S(2)}) async-start(bf16[8,128,128]{2,0,1:T(8,128)(2,1)} %copy.61), calls=%async_computation.3 | async-start | bytes 524288 | tf_op jit(solution)/shard_map/all_to_all | solution.py:180
  108.0 2.7 convolution_multiply_fusion.1
  111.8 7.3 %all-to-all-done.3 = bf16[8,128,128]{2,0,1:T(8,128)(2,1)} async-done(((bf16[8,128,128]{2,0,1:T(8,128)(2,1)}), bf16[8,128,128]{2,0,1:T(8,128)(2,1)}, u32[]{:S(2)}, u32[]{:S(2)}) %all-to-all-start.3) | async-done | bytes 262176 | tf_op jit(solution)/shard_map/all_to_all | solution.py:180
  119.1 4.4 %all-to-all-start.6 = ((bf16[8,128,128]{2,0,1:T(8,128)(2,1)}), bf16[8,128,128]{2,0,1:T(8,128)(2,1)}, u32[]{:S(2)}, u32[]{:S(2)}) async-start(bf16[8,128,128]{2,0,1:T(8,128)(2,1)} %copy.67), calls=%async_computation.6 | async-start | bytes 524288 | tf_op jit(solution)/shard_map/all_to_all | solution.py:216
  123.5 1.2 convolution_multiply_fusion
  125.8 8.6 %all-to-all-done.6 = bf16[8,128,128]{2,0,1:T(8,128)(2,1)} async-done(((bf16[8,128,128]{2,0,1:T(8,128)(2,1)}), bf16[8,128,128]{2,0,1:T(8,128)(2,1)}, u32[]{:S(2)}, u32[]{:S(2)}) %all-to-all-start.6) | async-done | bytes 262176 | tf_op jit(solution)/shard_map/all_to_all | solution.py:216
  134.4 3.5 %all-to-all-start.7 = ((bf16[8,128,128]{2,0,1:T(8,128)(2,1)}), bf16[8,128,128]{2,0,1:T(8,128)(2,1)S(1)}, u32[]{:S(2)}, u32[]{:S(2)}) async-start(bf16[8,128,128]{2,0,1:T(8,128)(2,1)} %copy.72), calls=%async_computation.7 | async-start | bytes 524288 | tf_op jit(solution)/shard_map/all_to_all | solution.py:219
  138.0 1.9 convolution_bitcast_fusion
  140.9 1.7 copy.62
  143.8 5.2 %all-to-all-done.7 = bf16[8,128,128]{2,0,1:T(8,128)(2,1)S(1)} async-done(((bf16[8,128,128]{2,0,1:T(8,128)(2,1)}), bf16[8,128,128]{2,0,1:T(8,128)(2,1)S(1)}, u32[]{:S(2)}, u32[]{:S(2)}) %all-to-all-start.7) | async-done | bytes 262176 | tf_op jit(solution)/shard_map/all_to_all | solution.py:219
  150.2 1.9 multiply_convert_fusion.2
  155.0 114.4 %all-reduce.2 = (bf16[4,128,128]{2,1,0:T(8,128)(2,1)}, bf16[2,128,128]{2,1,0:T(8,128)(2,1)}, bf16[128,512]{1,0:T(8,128)(2,1)}, bf16[512,128]{1,0:T(8,128)(2,1)},...) all-reduce(f32[4,128,128]{2,1,0:T(8,128)S(1)} %maximum_multiply_fus, ...), channel_id=1, replica_groups=mesh['dp'=32,'dap'=16] {'dp','dap'}, use_global_device_ids=true, to_apply=%region_12.0 | all-reduce | flops 229760 | bytes 1378560 | tf_op jit(solution)/shard_map/psum | solution.py:232
  270.1 2.0 fusion.46
  (133 shorter events, 22.6 us)
Async XLA Ops:
  0.6 78.1 %copy-start = (bf16[128,512]{1,0:T(8,128)(2,1)S(1)}, bf16[128,512]{1,0:T(8,128)(2,1)}, u32[]{:S(2)}) copy-start(bf16[128,512]{1,0:T(8,128)(2,1)} %param.14) | copy-start | bytes 393220
  1.4 5.8 %copy-start.30 = (f32[128]{0:T(128)}, f32[128]{0:T(128)S(1)}, u32[]{:S(2)}) copy-start(f32[128]{0:T(128)S(1)} %get-tuple-element.46) | copy-start | bytes 1540
  1.5 76.0 %copy-start.28 = (f32[128]{0:T(128)}, f32[128]{0:T(128)S(1)}, u32[]{:S(2)}) copy-start(f32[128]{0:T(128)S(1)} %get-tuple-element.47) | copy-start | bytes 1540
  1.5 79.7 %copy-start.33 = (f32[128]{0:T(128)}, f32[128]{0:T(128)S(1)}, u32[]{:S(2)}) copy-start(f32[128]{0:T(128)S(1)} %get-tuple-element.45) | copy-start | bytes 1540
  1.5 5.8 %copy-start.14 = (bf16[4,128,128]{2,1,0:T(8,128)(2,1)S(1)}, bf16[4,128,128]{2,1,0:T(8,128)(2,1)}, u32[]{:S(2)}) copy-start(bf16[4,128,128]{2,1,0:T(8,128)(2,1)} %param.12) | copy-start | bytes 393220
  7.6 12.6 %copy-start.8 = (f32[1024,128]{1,0:T(8,128)}, f32[1024,128]{1,0:T(8,128)S(1)}, u32[]{:S(2)}) copy-start(f32[1024,128]{1,0:T(8,128)S(1)} %fusion.12) | copy-start | bytes 1572868
  7.8 12.4 %copy-start.21 = (f32[1024]{0:T(1024)}, f32[1024]{0:T(1024)S(1)}, u32[]{:S(2)}) copy-start(f32[1024]{0:T(1024)S(1)} %multiply_bitcast_fusion) | copy-start | bytes 12292
  9.7 22.2 %all-to-all-start.1 = ((bf16[128,8,128]{2,1,0:T(8,128)(2,1)}), bf16[128,8,128]{2,1,0:T(8,128)(2,1)S(1)}, u32[]{:S(2)}, u32[]{:S(2)}) async-start(bf16[128,8,128]{2,1,0:T(8,128)(2,1)} %bitcast.17), calls=%async_computation.1 | async-start | bytes 524288 | tf_op jit(solution)/shard_map/all_to_all | solution.py:168
  31.9 43.7 %copy-start.2 = (bf16[128,8,128]{2,1,0:T(8,128)(2,1)}, bf16[128,8,128]{2,1,0:T(8,128)(2,1)S(1)}, u32[]{:S(2)}) copy-start(bf16[128,8,128]{2,1,0:T(8,128)(2,1)S(1)} %all-to-all-done.1) | copy-start | bytes 786436
  46.3 14.7 %all-to-all-start.4 = ((bf16[128,8,128]{2,1,0:T(8,128)(2,1)}), bf16[128,8,128]{2,1,0:T(8,128)(2,1)S(1)}, u32[]{:S(2)}, u32[]{:S(2)}) async-start(bf16[128,8,128]{2,1,0:T(8,128)(2,1)} %bitcast.33), calls=%async_computation.4 | async-start | bytes 524288 | tf_op jit(solution)/shard_map/all_to_all | solution.py:187
  61.0 14.6 %all-to-all-start.2 = ((bf16[8,128,128]{2,0,1:T(8,128)(2,1)}), bf16[8,128,128]{2,0,1:T(8,128)(2,1)S(1)}, u32[]{:S(2)}, u32[]{:S(2)}) async-start(bf16[8,128,128]{2,0,1:T(8,128)(2,1)} %copy.58), calls=%async_computation.2 | async-start | bytes 524288 | tf_op jit(solution)/shard_map/all_to_all | solution.py:173
  81.1 3.3 %copy-start.12 = (bf16[1024,512]{1,0:T(8,128)(2,1)}, bf16[1024,512]{1,0:T(8,128)(2,1)S(1)}, u32[]{:S(2)}) copy-start(bf16[1024,512]{1,0:T(8,128)(2,1)S(1)} %fusion.6) | copy-start | bytes 3145732
  81.1 3.3 %copy-start.18 = (bf16[2,128,128]{2,1,0:T(8,128)(2,1)S(1)}, bf16[2,128,128]{2,1,0:T(8,128)(2,1)}, u32[]{:S(2)}) copy-start(bf16[2,128,128]{2,1,0:T(8,128)(2,1)} %param.13) | copy-start | bytes 196612
  81.1 3.3 %copy-start.22 = (f32[1024]{0:T(1024)S(1)}, f32[1024]{0:T(1024)}, u32[]{:S(2)}) copy-start(f32[1024]{0:T(1024)} %get-tuple-element.41) | copy-start | bytes 12292
  81.2 3.3 %copy-start.23 = (f32[1024]{0:T(1024)S(1)}, f32[1024]{0:T(1024)}, u32[]{:S(2)}) copy-start(f32[1024]{0:T(1024)} %get-tuple-element.39) | copy-start | bytes 12292
  82.2 3.9 %copy-start.10 = (f32[1024,128]{1,0:T(8,128)}, f32[1024,128]{1,0:T(8,128)S(1)}, u32[]{:S(2)}) copy-start(f32[1024,128]{1,0:T(8,128)S(1)} %get-tuple-element.54) | copy-start | bytes 1572868
  82.2 3.9 %copy-start.24 = (f32[1024]{0:T(1024)}, f32[1024]{0:T(1024)S(1)}, u32[]{:S(2)}) copy-start(f32[1024]{0:T(1024)S(1)} %get-tuple-element.57) | copy-start | bytes 12292
  82.2 3.9 %copy-start.26 = (f32[1024]{0:T(1024)}, f32[1024]{0:T(1024)S(1)}, u32[]{:S(2)}) copy-start(f32[1024]{0:T(1024)S(1)} %get-tuple-element.58) | copy-start | bytes 12292
  84.4 8.3 %copy-start.5 = (bf16[1024,128]{1,0:T(8,128)(2,1)}, bf16[1024,128]{1,0:T(8,128)(2,1)S(1)}, u32[]{:S(2)}) copy-start(bf16[1024,128]{1,0:T(8,128)(2,1)S(1)} %get-tuple-element.25) | copy-start | bytes 786436
  89.2 14.6 %all-to-all-start.5 = ((bf16[128,8,128]{2,1,0:T(8,128)(2,1)}), bf16[128,8,128]{2,1,0:T(8,128)(2,1)S(1)}, u32[]{:S(2)}, u32[]{:S(2)}) async-start(bf16[128,8,128]{2,1,0:T(8,128)(2,1)} %bitcast.43), calls=%async_computation.5 | async-start | bytes 524288 | tf_op jit(solution)/shard_map/all_to_all | solution.py:205
  92.7 17.9 %copy-start.3 = (bf16[128,8,128]{2,1,0:T(8,128)(2,1)S(1)}, bf16[128,8,128]{2,1,0:T(8,128)(2,1)}, u32[]{:S(2)}) copy-start(bf16[128,8,128]{2,1,0:T(8,128)(2,1)} %copy-done.2) | copy-start | bytes 786436
  103.8 15.3 %all-to-all-start.3 = ((bf16[8,128,128]{2,0,1:T(8,128)(2,1)}), bf16[8,128,128]{2,0,1:T(8,128)(2,1)}, u32[]{:S(2)}, u32[]{:S(2)}) async-start(bf16[8,128,128]{2,0,1:T(8,128)(2,1)} %copy.61), calls=%async_computation.3 | async-start | bytes 524288 | tf_op jit(solution)/shard_map/all_to_all | solution.py:180
  111.8 26.2 %copy-start.6 = (bf16[1024,128]{1,0:T(8,128)(2,1)S(1)}, bf16[1024,128]{1,0:T(8,128)(2,1)}, u32[]{:S(2)}) copy-start(bf16[1024,128]{1,0:T(8,128)(2,1)} %copy-done.5) | copy-start | bytes 786436
  119.1 15.3 %all-to-all-start.6 = ((bf16[8,128,128]{2,0,1:T(8,128)(2,1)}), bf16[8,128,128]{2,0,1:T(8,128)(2,1)}, u32[]{:S(2)}, u32[]{:S(2)}) async-start(bf16[8,128,128]{2,0,1:T(8,128)(2,1)} %copy.67), calls=%async_computation.6 | async-start | bytes 524288 | tf_op jit(solution)/shard_map/all_to_all | solution.py:216
  123.5 16.3 %copy-start.4 = (bf16[1024,128]{1,0:T(8,128)(2,1)S(1)}, bf16[1024,128]{1,0:T(8,128)(2,1)}, u32[]{:S(2)}) copy-start(bf16[1024,128]{1,0:T(8,128)(2,1)} %get-tuple-element.26) | copy-start | bytes 786436
  124.7 15.1 %copy-start.19 = (bf16[2,128,128]{2,1,0:T(8,128)(2,1)S(1)}, bf16[2,128,128]{2,1,0:T(8,128)(2,1)}, u32[]{:S(2)}) copy-start(bf16[2,128,128]{2,1,0:T(8,128)(2,1)} %param.13) | copy-start | bytes 196612
  134.4 14.6 %all-to-all-start.7 = ((bf16[8,128,128]{2,0,1:T(8,128)(2,1)}), bf16[8,128,128]{2,0,1:T(8,128)(2,1)S(1)}, u32[]{:S(2)}, u32[]{:S(2)}) async-start(bf16[8,128,128]{2,0,1:T(8,128)(2,1)} %copy.72), calls=%async_computation.7 | async-start | bytes 524288 | tf_op jit(solution)/shard_map/all_to_all | solution.py:219
  153.8 116.3 %copy-start.11 = (f32[1024,128]{1,0:T(8,128)S(1)}, f32[1024,128]{1,0:T(8,128)}, u32[]{:S(2)}) copy-start(f32[1024,128]{1,0:T(8,128)} %copy-done.10) | copy-start | bytes 1572868
  154.1 116.0 %copy-start.25 = (f32[1024]{0:T(1024)S(1)}, f32[1024]{0:T(1024)}, u32[]{:S(2)}) copy-start(f32[1024]{0:T(1024)} %copy-done.24) | copy-start | bytes 12292
  154.1 116.0 %copy-start.27 = (f32[1024]{0:T(1024)S(1)}, f32[1024]{0:T(1024)}, u32[]{:S(2)}) copy-start(f32[1024]{0:T(1024)} %copy-done.26) | copy-start | bytes 12292
  154.1 116.0 %copy-start.32 = (f32[128]{0:T(128)S(1)}, f32[128]{0:T(128)}, u32[]{:S(2)}) copy-start(f32[128]{0:T(128)} %copy-done.30) | copy-start | bytes 1540
  154.1 116.0 %copy-start.34 = (f32[128]{0:T(128)S(1)}, f32[128]{0:T(128)}, u32[]{:S(2)}) copy-start(f32[128]{0:T(128)} %copy-done.33) | copy-start | bytes 1540
  (11 other events, 19.0 us)
where the time goes:
time: 274 us; the launch traced here: 272 us
  blocking collectives  129 us (47%)
  waiting for transfers between devices  60.2 us (22%)
  starting transfers between devices  32.9 us (12%)
  matrix products  20.4 us (7%)
  other arithmetic  17.5 us (6%)
  local copies, waits for them, and re-layouts  10.8 us (4%)
    psum x1, blocking collectives, local(): lax.psum((down_term, up_term, mid_gain_term, proj_term, out_term, pair_ga...  114 us
    all_to_all x1, blocking collectives, local(): lax.all_to_all(left_chan, 'dap', split_axis=0, concat_axis=1, tiled=True)  14.4 us
    dot_general x16, matrix products, matmul(): return jnp.dot(left_side, right_side, preferred_element_type=jnp.float32)  12.6 us
    all_to_all x1, waiting for transfers between devices, local(): lax.all_to_all(right_chan, 'dap', split_axis=0, concat_axis=1, tiled=True)  11.8 us
    all_to_all x1, waiting for transfers between devices, local(): lax.all_to_all(tri_part_chan.astype(jnp.bfloat16), 'dap', split_axis=1, c...  11 us
    all_to_all x1, starting transfers between devices, local(): lax.all_to_all(right_chan, 'dap', split_axis=0, concat_axis=1, tiled=True)  10.2 us
    all_to_all x1, waiting for transfers between devices, local(): lax.all_to_all(cotangent[0], 'dap', split_axis=0, concat_axis=1, tiled=True)  9.97 us
    all_to_all x1, waiting for transfers between devices, local(): lax.all_to_all(d_left_chan.astype(jnp.bfloat16), 'dap', split_axis=1, con...  8.58 us
  transfers between devices with their start and end apart: 7, of which 7 were waited for; matrix products, arithmetic and copies ran while one was open for 7% of the time, Pallas kernels for 0%

commit v1 on v0

v1 whole, which is shorter than its diff:
```python
import functools
import math

import jax
import jax.numpy as jnp
from jax import lax
from jax.experimental import pallas as pl
from jax.experimental.pallas import tpu as pltpu
from jax.sharding import PartitionSpec as P

EPSILON = 1e-05
GELU_SCALE = 0.7978845608028654
GELU_CUBIC = 0.044715
MESH = pl.DeviceIdType.MESH
F32 = jnp.float32
BF16 = jnp.bfloat16

C = 128
FFN = 512
ROWS = 8
PEERS = 16
PIECES = 4
PER = ROWS // PIECES
WIDE = PER * C
PACK = PER * 8
EARLY = 1536
LATE = 512


def dot(left, right):
    return jnp.dot(left, right, preferred_element_type=F32)


def dot_nt(left, right):
    return lax.dot_general(left, right, (((1,), (1,)), ((), ())), preferred_element_type=F32)


def dot_tn(left, right):
    return lax.dot_general(left, right, (((0,), (0,)), ((), ())), preferred_element_type=F32)


def norm(values):
    average = jnp.sum(values, axis=0, keepdims=True) * (1.0 / C)
    centred = values - average
    inv_std = lax.rsqrt(jnp.sum(centred * centred, axis=0, keepdims=True) * (1.0 / C) + EPSILON)
    return centred * inv_std, inv_std


def norm_back(incoming, normed, inv_std, gain):
    scaled = incoming * gain
    first = jnp.sum(scaled, axis=0, keepdims=True) * (1.0 / C)
    second = jnp.sum(scaled * normed, axis=0, keepdims=True) * (1.0 / C)
    return inv_std * (scaled - first - normed * second)


def wide(block):
    return jnp.concatenate([block] * PER, axis=1) if PER > 1 else block


def split_rows(values):
    parts = [values[:, r * C:(r + 1) * C].reshape(PEERS, 8, C) for r in range(PER)]
    return jnp.concatenate(parts, axis=1) if PER > 1 else parts[0]


def join_rows(chunks):
    parts = [chunks[:, r * 8:(r + 1) * 8, :].reshape(C, C) for r in range(PER)]
    return jnp.concatenate(parts, axis=1) if PER > 1 else parts[0]


def kernel(
    ndp, scale,
    pair, cot, mask_s, mask_v, gains, w_proj, w_out, w_up, w_down,
    out_next, out_grad, out_proj, out_out, out_up, out_down, out_gains,
    gain_b, wpT, woT, wuT, wdT, wcat,
    pairT, lnT, hat0, rstd0, ag, av, bg, bv,
    s_l, r_l, s_r, r_r, s_t, r_t, s_d, r_d, s_dl, r_dl, s_dr, r_dr, s_n, r_c,
    x_l, x_r, lc, rc, y_l, y_r,
    tri_ln, hid, mid_ln, d_pre, d_mid, d_stack, d_val, cotT,
    g_e, rs_e, ch_e, ex_e, fin_e, ag_e, g_f, rs_f, ch_f, ex_f, fin_f, ag_f,
    send, recv, once, once_send, red, red_send,
):
    me = lax.axis_index("dap")
    my_dp = lax.axis_index("dp")
    barrier = pltpu.get_barrier_semaphore()

    def hello_dap(t, _):
        pl.semaphore_signal(barrier, inc=1, device_id={"dap": lax.rem(me + t, PEERS)}, device_id_type=MESH)
        return 0

    def hello_dp(t, _):
        pl.semaphore_signal(barrier, inc=1, device_id={"dp": lax.rem(my_dp + t, ndp)}, device_id_type=MESH)
        return 0

    lax.fori_loop(1, PEERS, hello_dap, 0)
    lax.fori_loop(1, ndp, hello_dp, 0)

    for n in range(3):
        gain_b[n] = jnp.broadcast_to(gains[n:n + 1, :], (C, C)).T
    for m in range(4):
        w_m = w_proj[m]
        wpT[m * C:(m + 1) * C, :] = w_m.astype(F32).T.astype(BF16)
        wcat[:, m * C:(m + 1) * C] = w_m
        f_at = slice(m * C, (m + 1) * C)
        wuT[f_at, :] = w_up[:, f_at].astype(F32).T.astype(BF16)
        wdT[:, f_at] = w_down[f_at, :].astype(F32).T.astype(BF16)
    for m in range(2):
        woT[m] = w_out[m].astype(F32).T.astype(BF16)
    wcat[:, 4 * C:5 * C] = w_out[0]
    g_e[1280:EARLY, :] = jnp.zeros((EARLY - 1280, C), BF16)

    pl.semaphore_wait(barrier, PEERS - 1 + ndp - 1)

    def exchange(which, src, dst, p):
        def body(t, _):
            d = lax.rem(me + t, PEERS)
            pltpu.make_async_remote_copy(
                src_ref=src.at[p, d], dst_ref=dst.at[p, me],
                send_sem=send.at[which], recv_sem=recv.at[which, p],
                device_id={"dap": d}, device_id_type=MESH,
            ).start()
            return 0

        lax.fori_loop(1, PEERS, body, 0)
        dst[p, me] = src[p, me]

    def arrived(which, dst, p):
        ref = dst.at[p, pl.ds(0, PEERS - 1)]
        pltpu.make_async_copy(ref, ref, recv.at[which, p]).wait()

    def sent(which, src):
        ref = src.at[:, pl.ds(0, PEERS - 1)]
        pltpu.make_async_copy(ref, ref, send.at[which]).wait()

    def cot_body(t, _):
        d = lax.rem(me + t, PEERS)
        pltpu.make_async_remote_copy(
            src_ref=cot.at[pl.ds(pl.multiple_of(d * 64, 64), 64)], dst_ref=r_c.at[me],
            send_sem=once_send.at[0], recv_sem=once.at[0],
            device_id={"dap": d}, device_id_type=MESH,
        ).start()
        return 0

    lax.fori_loop(1, PEERS, cot_body, 0)
    own_cot = pltpu.make_async_copy(cot.at[pl.ds(pl.multiple_of(me * 64, 64), 64)], r_c.at[me], once.at[1])
    own_cot.start()

    mask_k = mask_v[...].astype(F32)

    def mask_of(p):
        parts = []
        for r in range(PER):
            m_i = mask_s[0, me * ROWS + p * PER + r].astype(F32)
            parts.append(mask_k * m_i)
        return jnp.concatenate(parts, axis=1) if PER > 1 else parts[0]

    def columns(p):
        return pl.ds(pl.multiple_of(p * WIDE, WIDE), WIDE)

    def front(p, _):
        at = columns(p)
        x_rows = pair[at, :].astype(F32)
        x = jnp.concatenate([x_rows[r * C:(r + 1) * C, :].T for r in range(PER)], axis=1) if PER > 1 else x_rows.T
        pairT[:, at] = x
        normed, inv_std = norm(x)
        hat0[:, at] = normed
        rstd0[:, at] = inv_std
        ln = (normed * wide(gain_b[0])).astype(BF16)
        lnT[:, at] = ln
        mask = mask_of(p)
        gate = jax.nn.sigmoid(dot(wpT[0:C, :], ln))
        value = dot(wpT[C:2 * C, :], ln)
        ag[:, at] = gate
        av[:, at] = value
        s_l[p] = split_rows(mask * gate * value).astype(BF16)
        exchange(0, s_l, r_l, p)
        gate = jax.nn.sigmoid(dot(wpT[2 * C:3 * C, :], ln))
        value = dot(wpT[3 * C:4 * C, :], ln)
        bg[:, at] = gate
        bv[:, at] = value
        s_r[p] = split_rows(mask * gate * value).astype(BF16)
        exchange(1, s_r, r_r, p)
        return 0

    lax.fori_loop(0, PIECES, front, 0)

    def spread(dst, src, p):
        for s in range(PEERS):
            dst[pl.ds(pl.multiple_of(s * 64 + p * PACK, PACK), PACK), :] = src[p, s].astype(F32)

    def gather_chunks(p):
        return lambda ref: jnp.stack(
            [ref[pl.ds(pl.multiple_of(s * 64 + p * PACK, PACK), PACK), :] for s in range(PEERS)]
        ).astype(BF16)

    def take_l(p, _):
        arrived(0, r_l, p)
        spread(x_l, r_l, p)
        arrived(1, r_r, p)
        spread(x_r, r_r, p)
        return 0

    lax.fori_loop(0, PIECES, take_l, 0)

    def tri_body(c, _):
        left = x_l[pl.ds(c, C, 8), :].astype(BF16)
        right = x_r[pl.ds(c, C, 8), :].astype(BF16)
        lc[c] = left
        rc[c] = right
        y_l[pl.ds(c, C, 8), :] = dot_nt(left, right)
        return 0

    lax.fori_loop(0, 8, tri_body, 0)

    def tri_send(p, _):
        s_t[p] = gather_chunks(p)(y_l)
        exchange(2, s_t, r_t, p)
        return 0

    lax.fori_loop(0, PIECES, tri_send, 0)

    own_cot.wait()
    all_cot = r_c.at[pl.ds(0, PEERS - 1)]
    pltpu.make_async_copy(all_cot, all_cot, once.at[0]).wait()

    def next_body(p):
        rows = pl.ds(pl.multiple_of(me * 64 + p * PACK, PACK), PACK)

        def body(t, _):
            d = lax.rem(me + t, PEERS)
            pltpu.make_async_remote_copy(
                src_ref=s_n.at[p, d], dst_ref=out_next.at[rows],
                send_sem=once_send.at[1], recv_sem=once.at[2],
                device_id={"dap": d}, device_id_type=MESH,
            ).start()
            return 0

        lax.fori_loop(1, PEERS, body, 0)
        pltpu.make_async_copy(s_n.at[p, me], out_next.at[rows], once.at[3]).start()

    def middle(p, _):
        at = columns(p)
        arrived(2, r_t, p)
        tri = join_rows(r_t[p].astype(F32))
        tri_hat, tri_rstd = norm(tri)
        t_ln = (tri_hat * wide(gain_b[1])).astype(BF16)
        tri_ln[:, at] = t_ln
        out_gate = jax.nn.sigmoid(dot(woT[0], lnT[:, at]))
        out_value = dot(woT[1], t_ln)
        mid = (pairT[:, at] + out_gate * out_value).astype(BF16).astype(F32)
        mid_hat, mid_rstd = norm(mid)
        m_ln = (mid_hat * wide(gain_b[2])).astype(BF16)
        mid_ln[:, at] = m_ln
        cot_rows = r_c[:, pl.ds(pl.multiple_of(p * PACK, PACK), PACK), :].astype(F32)
        cot_t = jnp.concatenate(
            [cot_rows[:, r * 8:(r + 1) * 8, :].reshape(C, C).T for r in range(PER)], axis=1
        )
        cot_b = cot_t.astype(BF16)
        cotT[:, at] = cot_b
        for f in range(4):
            f_at = slice(f * C, (f + 1) * C)
            u = dot(wuT[f_at, :], m_ln)
            square = u * u
            tanh = jnp.tanh(u * (GELU_SCALE + GELU_SCALE * GELU_CUBIC * square))
            half = 0.5 + 0.5 * tanh
            act = u * half
            slope = half + act * (1.0 - tanh) * (GELU_SCALE + 3.0 * GELU_SCALE * GELU_CUBIC * square)
            hid[f_at, at] = act.astype(BF16)
            d_pre[f_at, at] = (dot(w_down[f_at, :], cot_b) * slope).astype(BF16)
        d_mid_v = cot_t + norm_back(dot(w_up[...], d_pre[:, at]), mid_hat, mid_rstd, wide(gain_b[2]))
        d_mid[:, at] = d_mid_v
        d_gate = (d_mid_v * out_value * out_gate * (1.0 - out_gate)).astype(BF16)
        d_stack[4 * C:5 * C, at] = d_gate
        d_value = (d_mid_v * out_gate).astype(BF16)
        d_val[:, at] = d_value
        d_tri = norm_back(dot(w_out[1], d_value), tri_hat, tri_rstd, wide(gain_b[1]))
        s_d[p] = split_rows(d_tri).astype(BF16)
        exchange(3, s_d, r_d, p)
        nxt = mid + dot(wdT[...], hid[:, at])
        nxt_rows = jnp.concatenate(
            [nxt[:, r * C:(r + 1) * C].T.reshape(PEERS, 8, C) for r in range(PER)], axis=1
        )
        s_n[p] = nxt_rows.astype(BF16)
        next_body(p)
        return 0

    lax.fori_loop(0, PIECES, middle, 0)

    def reduce_scatter(which, src, dst, rows):
        def body(t, _):
            q = lax.rem(my_dp + t, ndp)
            pltpu.make_async_remote_copy(
                src_ref=src.at[pl.ds(pl.multiple_of(q * rows, 16), rows)], dst_ref=dst.at[my_dp],
                send_sem=red_send.at[which], recv_sem=red.at[which],
                device_id={"dp": q}, device_id_type=MESH,
            ).start()
            return 0

        lax.fori_loop(1, ndp, body, 0)
        dst[my_dp] = src[pl.ds(pl.multiple_of(my_dp * rows, 16), rows), :]

    def wait_count(ref, sem):
        pltpu.make_async_copy(ref, ref, sem).wait()

    def total(ref, count):
        def body(n, value):
            return value + ref[n].astype(F32)

        return lax.fori_loop(1, count, body, ref[0].astype(F32))

    def cross(which, src, dst):
        def body(t, _):
            d = lax.rem(me + t, PEERS)
            pltpu.make_async_remote_copy(
                src_ref=src, dst_ref=dst.at[me],
                send_sem=red_send.at[which], recv_sem=red.at[which],
                device_id={"dap": d}, device_id_type=MESH,
            ).start()
            return 0

        lax.fori_loop(1, PEERS, body, 0)
        dst[me] = src[...]

    def all_gather(which, src, dst, rows):
        place = pl.ds(pl.multiple_of(my_dp * rows, 16), rows)

        def body(t, _):
            q = lax.rem(my_dp + t, ndp)
            pltpu.make_async_remote_copy(
                src_ref=src, dst_ref=dst.at[place],
                send_sem=red_send.at[which], recv_sem=red.at[which],
                device_id={"dp": q}, device_id_type=MESH,
            ).start()
            return 0

        lax.fori_loop(1, ndp, body, 0)
        dst[place, :] = src[...]

    rows_e, rows_f = EARLY // ndp, LATE // ndp

    for f in range(4):
        f_at = slice(f * C, (f + 1) * C)
        g_e[f_at, :] = dot_nt(mid_ln[...], d_pre[f_at, :]).astype(BF16)
        g_e[512 + f * C:512 + (f + 1) * C, :] = dot_nt(hid[f_at, :], cotT[...]).astype(BF16)
    g_e[1024:1152, :] = dot_nt(lnT[...], d_stack[4 * C:5 * C, :]).astype(BF16)
    g_e[1152:1280, :] = dot_nt(tri_ln[...], d_val[...]).astype(BF16)
    reduce_scatter(0, g_e, rs_e, rows_e)

    def take_d(p, _):
        arrived(3, r_d, p)
        spread(x_l, r_d, p)
        return 0

    lax.fori_loop(0, PIECES, take_d, 0)

    def back_body(c, _):
        grad = x_l[pl.ds(c, C, 8), :].astype(BF16)
        y_l[pl.ds(c, C, 8), :] = dot(grad, rc[c])
        y_r[pl.ds(c, C, 8), :] = dot_tn(grad, lc[c])
        return 0

    lax.fori_loop(0, 8, back_body, 0)

    def back_send(p, _):
        s_dl[p] = gather_chunks(p)(y_l)
        exchange(4, s_dl, r_dl, p)
        s_dr[p] = gather_chunks(p)(y_r)
        exchange(5, s_dr, r_dr, p)
        return 0

    lax.fori_loop(0, PIECES, back_send, 0)

    wait_count(rs_e.at[pl.ds(0, ndp - 1)], red.at[0])
    ch_e[...] = total(rs_e, ndp).astype(BF16)
    cross(1, ch_e, ex_e)

    def lower(p, _):
        at = columns(p)
        mask = mask_of(p)
        arrived(4, r_dl, p)
        grad = join_rows(r_dl[p].astype(F32)) * mask
        gate = ag[:, at]
        with_gate = grad * gate
        d_stack[0:C, at] = (with_gate * av[:, at] * (1.0 - gate)).astype(BF16)
        d_stack[C:2 * C, at] = with_gate.astype(BF16)
        arrived(5, r_dr, p)
        grad = join_rows(r_dr[p].astype(F32)) * mask
        gate = bg[:, at]
        with_gate = grad * gate
        d_stack[2 * C:3 * C, at] = (with_gate * bv[:, at] * (1.0 - gate)).astype(BF16)
        d_stack[3 * C:4 * C, at] = with_gate.astype(BF16)
        d_ln = dot(wcat[...], d_stack[:, at])
        result = d_mid[:, at] + norm_back(d_ln, hat0[:, at], rstd0[:, at], wide(gain_b[0]))
        for r in range(PER):
            row = pl.ds(pl.multiple_of(p * WIDE + r * C, C), C)
            out_grad[row, :] = result[:, r * C:(r + 1) * C].T.astype(BF16)
        return 0

    lax.fori_loop(0, PIECES, lower, 0)

    for m in range(4):
        m_at = slice(m * C, (m + 1) * C)
        g_f[m_at, :] = dot_nt(lnT[...], d_stack[m_at, :]).astype(BF16)
    reduce_scatter(2, g_f, rs_f, rows_f)

    wait_count(ex_e.at[pl.ds(0, PEERS - 1)], red.at[1])
    fin_e[...] = (total(ex_e, PEERS) * scale).astype(BF16)
    all_gather(4, fin_e, ag_e, rows_e)

    wait_count(rs_f.at[pl.ds(0, ndp - 1)], red.at[2])
    ch_f[...] = total(rs_f, ndp).astype(BF16)
    cross(3, ch_f, ex_f)
    wait_count(ex_f.at[pl.ds(0, PEERS - 1)], red.at[3])
    fin_f[...] = (total(ex_f, PEERS) * scale).astype(BF16)
    all_gather(5, fin_f, ag_f, rows_f)

    wait_count(ag_e.at[pl.ds(0, (ndp - 1) * rows_e)], red.at[4])
    mid_sum = jnp.zeros((C, C), F32)
    for f in range(4):
        f_at = slice(f * C, (f + 1) * C)
        block = ag_e[f_at, :]
        out_up[:, f_at] = block
        mid_sum = mid_sum + block.astype(F32) * w_up[:, f_at].astype(F32)
    out_down[...] = ag_e[512:1024, :]
    out_out[...] = ag_e[1024:1280, :]
    pair_sum = ag_e[1024:1152, :].astype(F32) * w_out[0].astype(F32)
    tri_sum = ag_e[1152:1280, :].astype(F32) * w_out[1].astype(F32)

    wait_count(ag_f.at[pl.ds(0, (ndp - 1) * rows_f)], red.at[5])
    for m in range(4):
        block = ag_f[m * C:(m + 1) * C, :]
        pair_sum = pair_sum + block.astype(F32) * w_proj[m].astype(F32)
    out_proj[...] = ag_f[...]
    sums = [jnp.sum(s.T, axis=0, keepdims=True) for s in (pair_sum, tri_sum, mid_sum)]
    out_gains[...] = (jnp.concatenate(sums, axis=0) / gains[...]).astype(BF16)

    for which, src in enumerate((s_l, s_r, s_t, s_d, s_dl, s_dr)):
        sent(which, src)
    sent_cot = r_c.at[pl.ds(0, PEERS - 1)]
    wait_count(sent_cot, once_send.at[0])
    all_next = s_n.at[:, pl.ds(0, PEERS - 1)]
    wait_count(all_next, once_send.at[1])
    wait_count(all_next, once.at[2])
    wait_count(s_n.at[:, 0], once.at[3])
    wait_count(rs_e.at[pl.ds(0, ndp - 1)], red_send.at[0])
    wait_count(ex_e.at[pl.ds(0, PEERS - 1)], red_send.at[1])
    wait_count(rs_f.at[pl.ds(0, ndp - 1)], red_send.at[2])
    wait_count(ex_f.at[pl.ds(0, PEERS - 1)], red_send.at[3])
    wait_count(ag_e.at[pl.ds(0, (ndp - 1) * rows_e)], red_send.at[4])
    wait_count(ag_f.at[pl.ds(0, (ndp - 1) * rows_f)], red_send.at[5])


def local(ndp, pair_repr, cotangent, residue_mask, norm_gains, w_proj, w_out, w_up, w_down):
    scale = 1.0 / math.sqrt(ndp * C * C)
    vmem = pl.BlockSpec(memory_space=pltpu.VMEM)
    smem = pl.BlockSpec(memory_space=pltpu.SMEM)
    hbm = pl.BlockSpec(memory_space=pl.ANY)
    columns = ROWS * C
    chunks = pltpu.VMEM((PIECES, PEERS, PACK, C), BF16)
    full = pltpu.VMEM((C, columns), F32)
    half = pltpu.VMEM((C, columns), BF16)
    big = pltpu.VMEM((FFN, columns), BF16)
    cube = pltpu.VMEM((1024, C), F32)
    rows_e, rows_f = EARLY // ndp, LATE // ndp
    scratch = [
        pltpu.VMEM((3, C, C), F32),
        pltpu.VMEM((4 * C, C), BF16),
        pltpu.VMEM((2, C, C), BF16),
        pltpu.VMEM((FFN, C), BF16),
        pltpu.VMEM((C, FFN), BF16),
        pltpu.VMEM((C, 5 * C), BF16),
        full, half, full, pltpu.VMEM((1, columns), F32), full, full, full, full,
        *([chunks] * 13),
        pltpu.VMEM((PEERS, 64, C), BF16),
        cube, cube, pltpu.VMEM((8, C, C), BF16), pltpu.VMEM((8, C, C), BF16), cube, cube,
        half, big, half, big, full, pltpu.VMEM((5 * C, columns), BF16), half, half,
    ]
    for rows, whole in ((rows_e, EARLY), (rows_f, LATE)):
        scratch += [
            pltpu.VMEM((whole, C), BF16),
            pltpu.VMEM((ndp, rows, C), BF16),
            pltpu.VMEM((rows, C), BF16),
            pltpu.VMEM((PEERS, rows, C), BF16),
            pltpu.VMEM((rows, C), BF16),
            pltpu.VMEM((whole, C), BF16),
        ]
    scratch += [
        pltpu.SemaphoreType.DMA((6,)),
        pltpu.SemaphoreType.DMA((6, PIECES)),
        pltpu.SemaphoreType.DMA((4,)),
        pltpu.SemaphoreType.DMA((2,)),
        pltpu.SemaphoreType.DMA((6,)),
        pltpu.SemaphoreType.DMA((6,)),
    ]
    results = pl.pallas_call(
        functools.partial(kernel, ndp, scale),
        out_shape=(
            jax.ShapeDtypeStruct((1024, C), BF16),
            jax.ShapeDtypeStruct((1024, C), BF16),
            jax.ShapeDtypeStruct((4 * C, C), BF16),
            jax.ShapeDtypeStruct((2 * C, C), BF16),
            jax.ShapeDtypeStruct((C, FFN), BF16),
            jax.ShapeDtypeStruct((FFN, C), BF16),
            jax.ShapeDtypeStruct((3, C), BF16),
        ),
        in_specs=[vmem, hbm, smem, vmem, vmem, vmem, vmem, vmem, vmem],
        out_specs=(hbm, vmem, vmem, vmem, vmem, vmem, vmem),
        scratch_shapes=scratch,
        compiler_params=pltpu.CompilerParams(
            collective_id=0, has_side_effects=True, vmem_limit_bytes=48 * 1024 * 1024
        ),
        cost_estimate=pl.CostEstimate(flops=1_600_000_000, bytes_accessed=3_000_000, transcendentals=1_200_000),
    )(
        pair_repr.reshape(1024, C), cotangent.reshape(1024, C), residue_mask, residue_mask,
        norm_gains, w_proj, w_out, w_up, w_down,
    )
    nxt, grad, g_proj, g_out, g_up, g_down, g_gains = results
    return (
        nxt.reshape(1, C, ROWS, C),
        grad.reshape(1, ROWS, C, C),
        g_proj.reshape(4, C, C),
        g_out.reshape(2, C, C),
        g_up,
        g_down,
        g_gains,
    )


def solution(mesh):
    in_specs = (
        P("dp", "dap", None, None),
        P("dp", None, "dap", None),
        P("dp", None),
        P(),
        P(),
        P(),
        P(),
        P(),
    )
    out_specs = (P("dp", None, "dap", None), P("dp", "dap", None, None), P(), P(), P(), P(), P())
    body = functools.partial(local, mesh.shape["dp"])
    return jax.shard_map(body, mesh=mesh, in_specs=in_specs, out_specs=out_specs, check_vma=False)
```

time: 274 us -> 109 us (0.40)
  blocking collectives: 129 us -> 0 us
  Pallas kernels: 0 us -> 97.4 us
  waiting for transfers between devices: 60.2 us -> 0 us
  starting transfers between devices: 32.9 us -> 0 us
  matrix products: 20.4 us -> 0 us
  other arithmetic: 17.5 us -> 0 us
    psum x1 -> x0, blocking collectives: 114 us -> none  [local(): lax.psum((down_term, up_term, mid_gain_term, proj_term, out_term, pair_ga...]
    pallas_call x0 -> x1, Pallas kernels: none -> 97.4 us  [local(): pl.pallas_call(functools.partial(kernel, ndp, scale), out_shape=(jax.Shap...]
    all_to_all x7 -> x0, waiting for transfers between devices: 60.2 us -> none  [the longest x1 11.8 us: local(): lax.all_to_all(right_chan, 'dap', split_axis=0, concat_axis=1, tiled=True)]
    all_to_all x7 -> x0, starting transfers between devices: 32.9 us -> none  [the longest x1 10.2 us: local(): lax.all_to_all(right_chan, 'dap', split_axis=0, concat_axis=1, tiled=True)]
    dot_general x27 -> x0, matrix products: 20.4 us -> none  [the longest x16 12.6 us: matmul(): return jnp.dot(left_side, right_side, preferred_element_type=jnp.float32)]
    all_to_all x1 -> x0, blocking collectives: 14.4 us -> none  [local(): lax.all_to_all(left_chan, 'dap', split_axis=0, concat_axis=1, tiled=True)]
    unnamed x72 -> x23, local copies, waits for them, and re-layouts: 0.17 us -> 10.7 us
    convert_element_type x7 -> x0, other arithmetic: 8.99 us -> none  [the longest x1 2.22 us: upper_back(): d_value = (d_mid * out_gate).astype(jnp.bfloat16)]
  transfers between devices with their start and end apart: 7 -> 0, of which waited for: 7 -> 0; matrix products, arithmetic and copies ran while one was open for 7% -> 0% of each run, Pallas kernels for 0% -> 0%
where the time goes in v1:
time: 109 us
  Pallas kernels  97.4 us (89%)
  local copies, waits for them, and re-layouts  10.7 us (10%)
    pallas_call x1, Pallas kernels, local(): pl.pallas_call(functools.partial(kernel, ndp, scale), out_shape=(jax.Shap...  97.4 us
    unnamed x23, local copies, waits for them, and re-layouts  10.7 us

profile of v1, /device:TPU:1, one launch (start us, length us, event | category | flops | bytes accessed | tf_op | source)
XLA Modules:
  0.0 108.8 jit_solution(15642284747284600275)
XLA Ops:
  0.6 0.0 copy-start.6
  0.6 0.0 copy-start.7
  0.7 0.7 copy-done.6
  1.3 0.0 copy-done.7
  1.3 0.0 copy-start
  1.3 0.9 copy-done
  2.3 0.0 copy-start.1
  2.3 0.9 copy-done.1
  3.2 0.0 copy-start.2
  3.2 0.9 copy-done.2
  4.1 0.0 copy-start.3
  4.1 0.9 copy-done.3
  5.0 0.0 copy-start.4
  5.0 0.9 copy-done.4
  5.9 0.0 copy-start.5
  5.9 0.8 copy-done.5
  6.8 97.4 %shard_map.135 = (bf16[1024,128]{1,0:T(8,128)(2,1)S(1)}, bf16[1024,128]{1,0:T(8,128)(2,1)S(1)}, bf16[512,128]{1,0:T(8,128)(2,1)S(1)}, bf16[256,128]{1,0:T(8,128)...) custom-call(bf16[1024,128]{1,0:T(8,128)(2,1)S(1)} %bitcast.10, ...), custom_call_target="tpu_custom_call" | custom-call | flops 1600000000 | bytes 3000000 | tf_op jit(solution)/shard_map/pallas_call | solution.py:494
  104.2 0.7 copy.22
  104.9 0.7 copy.23
  105.6 0.7 copy.24
  106.3 0.6 copy.25
  106.9 0.7 copy.26
  107.6 0.7 copy.27
  108.2 0.6 copy.28
Async XLA Ops:
  0.6 0.7 copy-start.6
  0.6 0.7 copy-start.7
  1.3 1.0 copy-start
  2.3 0.9 copy-start.1
  3.2 0.9 copy-start.2
  4.1 0.9 copy-start.3
  5.0 0.9 copy-start.4
  5.9 0.8 copy-start.5

commit v2 on v1

--- a/solution.py
+++ b/solution.py
@@ -27,6 +27,18 @@
 LATE = 512
 
 
+AWAY = sorted(
+    [(dy, dx) for dy in range(-3, 5) for dx in range(2) if dy or dx],
+    key=lambda at: (-abs(at[0]) - 2 * at[1], at[0]),
+)
+
+
+def far_crops(ndp):
+    depth = max(1, ndp // 4)
+    steps = [(dz, dr) for dz in range(-((depth - 1) // 2), depth // 2 + 1) for dr in range(ndp // depth) if dz or dr]
+    return sorted(steps, key=lambda at: (-abs(at[0]) - at[1] // 2, -at[1], at[0]))
+
+
 def dot(left, right):
     return jnp.dot(left, right, preferred_element_type=F32)
 
@@ -69,9 +81,11 @@
 
 def kernel(
     ndp, scale,
-    pair, cot, mask_s, mask_v, gains, w_proj, w_out, w_up, w_down,
-    out_next, out_grad, out_proj, out_out, out_up, out_down, out_gains,
-    gain_b, wpT, woT, wuT, wdT, wcat,
+    pair_h, cot, mask_h, gains_h, w_proj_h, w_out_h, w_up_h, w_down_h,
+    out_next, out_grad_h, out_proj_h, out_out_h, out_up_h, out_down_h, out_gains_h,
+    pair, mask_v, gains, w_proj, w_out, w_up, w_down,
+    out_grad, out_proj, out_out, out_up, out_down, out_gains, in_sem, out_sem,
+    mask_b, gain_b, wpT, woT, wuT, wdT, wcat,
     pairT, lnT, hat0, rstd0, ag, av, bg, bv,
     s_l, r_l, s_r, r_r, s_t, r_t, s_d, r_d, s_dl, r_dl, s_dr, r_dr, s_n, r_c,
     x_l, x_r, lc, rc, y_l, y_r,
@@ -83,44 +97,56 @@
     my_dp = lax.axis_index("dp")
     barrier = pltpu.get_barrier_semaphore()
 
-    def hello_dap(t, _):
-        pl.semaphore_signal(barrier, inc=1, device_id={"dap": lax.rem(me + t, PEERS)}, device_id_type=MESH)
-        return 0
-
-    def hello_dp(t, _):
-        pl.semaphore_signal(barrier, inc=1, device_id={"dp": lax.rem(my_dp + t, ndp)}, device_id_type=MESH)
-        return 0
-
-    lax.fori_loop(1, PEERS, hello_dap, 0)
-    lax.fori_loop(1, ndp, hello_dp, 0)
-
+    def peer(dy, dx):
+        return lax.rem(me // 2 + dy + 8, 8) * 2 + lax.rem(me + dx, 2)
+
+    depth = max(1, ndp // 4)
+    near = ndp // depth
+    crops = far_crops(ndp)
+
+    def crop(dz, dr):
+        here = lax.rem(my_dp, near)
+        if near == 4:
+            there = lax.rem(here // 2 + dr // 2, 2) * 2 + lax.rem(here + dr, 2)
+        else:
+            there = lax.rem(here + dr, near)
+        return lax.rem(my_dp // near + dz + depth, depth) * near + there
+
+    for dy, dx in AWAY:
+        pl.semaphore_signal(barrier, inc=1, device_id={"dap": peer(dy, dx)}, device_id_type=MESH)
+    for dz, dr in crops:
+        pl.semaphore_signal(barrier, inc=1, device_id={"dp": crop(dz, dr)}, device_id_type=MESH)
+
+    loads = [
+        pltpu.make_async_copy(src, dst, in_sem.at[n])
+        for n, (src, dst) in enumerate((
+            (pair_h, pair), (mask_h, mask_v), (gains_h, gains), (w_proj_h, w_proj),
+            (w_out_h, w_out), (w_up_h, w_up), (w_down_h, w_down),
+        ))
+    ]
+    for load in loads:
+        load.start()
+    for load in loads[1:4]:
+        load.wait()
+
+    mask_k = mask_v[...].astype(F32)
+    mask_b[...] = jnp.broadcast_to(mask_k, (C, C)).T
     for n in range(3):
         gain_b[n] = jnp.broadcast_to(gains[n:n + 1, :], (C, C)).T
     for m in range(4):
         w_m = w_proj[m]
         wpT[m * C:(m + 1) * C, :] = w_m.astype(F32).T.astype(BF16)
         wcat[:, m * C:(m + 1) * C] = w_m
-        f_at = slice(m * C, (m + 1) * C)
-        wuT[f_at, :] = w_up[:, f_at].astype(F32).T.astype(BF16)
-        wdT[:, f_at] = w_down[f_at, :].astype(F32).T.astype(BF16)
-    for m in range(2):
-        woT[m] = w_out[m].astype(F32).T.astype(BF16)
-    wcat[:, 4 * C:5 * C] = w_out[0]
-    g_e[1280:EARLY, :] = jnp.zeros((EARLY - 1280, C), BF16)
-
-    pl.semaphore_wait(barrier, PEERS - 1 + ndp - 1)
+    loads[0].wait()
 
     def exchange(which, src, dst, p):
-        def body(t, _):
-            d = lax.rem(me + t, PEERS)
+        for dy, dx in AWAY:
+            d = peer(dy, dx)
             pltpu.make_async_remote_copy(
                 src_ref=src.at[p, d], dst_ref=dst.at[p, me],
                 send_sem=send.at[which], recv_sem=recv.at[which, p],
                 device_id={"dap": d}, device_id_type=MESH,
             ).start()
-            return 0
-
-        lax.fori_loop(1, PEERS, body, 0)
         dst[p, me] = src[p, me]
 
     def arrived(which, dst, p):
@@ -131,32 +157,16 @@
         ref = src.at[:, pl.ds(0, PEERS - 1)]
         pltpu.make_async_copy(ref, ref, send.at[which]).wait()
 
-    def cot_body(t, _):
-        d = lax.rem(me + t, PEERS)
-        pltpu.make_async_remote_copy(
-            src_ref=cot.at[pl.ds(pl.multiple_of(d * 64, 64), 64)], dst_ref=r_c.at[me],
-            send_sem=once_send.at[0], recv_sem=once.at[0],
-            device_id={"dap": d}, device_id_type=MESH,
-        ).start()
-        return 0
-
-    lax.fori_loop(1, PEERS, cot_body, 0)
-    own_cot = pltpu.make_async_copy(cot.at[pl.ds(pl.multiple_of(me * 64, 64), 64)], r_c.at[me], once.at[1])
-    own_cot.start()
-
-    mask_k = mask_v[...].astype(F32)
-
     def mask_of(p):
         parts = []
         for r in range(PER):
-            m_i = mask_s[0, me * ROWS + p * PER + r].astype(F32)
-            parts.append(mask_k * m_i)
+            parts.append(mask_k * mask_b[pl.ds(me * ROWS + p * PER + r, 1), :])
         return jnp.concatenate(parts, axis=1) if PER > 1 else parts[0]
 
     def columns(p):
         return pl.ds(pl.multiple_of(p * WIDE, WIDE), WIDE)
 
-    def front(p, _):
+    def front(p):
         at = columns(p)
         x_rows = pair[at, :].astype(F32)
         x = jnp.concatenate([x_rows[r * C:(r + 1) * C, :].T for r in range(PER)], axis=1) if PER > 1 else x_rows.T
@@ -172,16 +182,46 @@
         ag[:, at] = gate
         av[:, at] = value
         s_l[p] = split_rows(mask * gate * value).astype(BF16)
-        exchange(0, s_l, r_l, p)
         gate = jax.nn.sigmoid(dot(wpT[2 * C:3 * C, :], ln))
         value = dot(wpT[3 * C:4 * C, :], ln)
         bg[:, at] = gate
         bv[:, at] = value
         s_r[p] = split_rows(mask * gate * value).astype(BF16)
+
+    def front_send(p):
+        exchange(0, s_l, r_l, p)
         exchange(1, s_r, r_r, p)
-        return 0
-
-    lax.fori_loop(0, PIECES, front, 0)
+
+    def front_step(p, _):
+        front_send(p)
+        front(p + 1)
+        return 0
+
+    front(0)
+    pl.semaphore_wait(barrier, PEERS - 1 + ndp - 1)
+    lax.fori_loop(0, PIECES - 1, front_step, 0)
+    front_send(PIECES - 1)
+
+    for dy, dx in AWAY:
+        d = peer(dy, dx)
+        pltpu.make_async_remote_copy(
+            src_ref=cot.at[pl.ds(pl.multiple_of(d * 64, 64), 64)], dst_ref=r_c.at[me],
+            send_sem=once_send.at[0], recv_sem=once.at[0],
+            device_id={"dap": d}, device_id_type=MESH,
+        ).start()
+    own_cot = pltpu.make_async_copy(cot.at[pl.ds(pl.multiple_of(me * 64, 64), 64)], r_c.at[me], once.at[1])
+    own_cot.start()
+
+    for load in loads[4:]:
+        load.wait()
+    for m in range(4):
+        f_at = slice(m * C, (m + 1) * C)
+        wuT[f_at, :] = w_up[:, f_at].astype(F32).T.astype(BF16)
+        wdT[:, f_at] = w_down[f_at, :].astype(F32).T.astype(BF16)
+    for m in range(2):
+        woT[m] = w_out[m].astype(F32).T.astype(BF16)
+    wcat[:, 4 * C:5 * C] = w_out[0]
+    g_e[1280:EARLY, :] = jnp.zeros((EARLY - 1280, C), BF16)
 
     def spread(dst, src, p):
         for s in range(PEERS):
@@ -225,16 +265,13 @@
     def next_body(p):
         rows = pl.ds(pl.multiple_of(me * 64 + p * PACK, PACK), PACK)
 
-        def body(t, _):
-            d = lax.rem(me + t, PEERS)
+        for dy, dx in AWAY:
+            d = peer(dy, dx)
             pltpu.make_async_remote_copy(
                 src_ref=s_n.at[p, d], dst_ref=out_next.at[rows],
                 send_sem=once_send.at[1], recv_sem=once.at[2],
                 device_id={"dap": d}, device_id_type=MESH,
             ).start()
-            return 0
-
-        lax.fori_loop(1, PEERS, body, 0)
         pltpu.make_async_copy(s_n.at[p, me], out_next.at[rows], once.at[3]).start()
 
     def middle(p, _):
@@ -280,22 +317,24 @@
             [nxt[:, r * C:(r + 1) * C].T.reshape(PEERS, 8, C) for r in range(PER)], axis=1
         )
         s_n[p] = nxt_rows.astype(BF16)
+        return 0
+
+    lax.fori_loop(0, PIECES, middle, 0)
+
+    def send_next(p, _):
         next_body(p)
         return 0
 
-    lax.fori_loop(0, PIECES, middle, 0)
+    lax.fori_loop(0, PIECES, send_next, 0)
 
     def reduce_scatter(which, src, dst, rows):
-        def body(t, _):
-            q = lax.rem(my_dp + t, ndp)
+        for dz, dr in crops:
+            q = crop(dz, dr)
             pltpu.make_async_remote_copy(
                 src_ref=src.at[pl.ds(pl.multiple_of(q * rows, 16), rows)], dst_ref=dst.at[my_dp],
                 send_sem=red_send.at[which], recv_sem=red.at[which],
                 device_id={"dp": q}, device_id_type=MESH,
             ).start()
-            return 0
-
-        lax.fori_loop(1, ndp, body, 0)
         dst[my_dp] = src[pl.ds(pl.multiple_of(my_dp * rows, 16), rows), :]
 
     def wait_count(ref, sem):
@@ -308,31 +347,23 @@
         return lax.fori_loop(1, count, body, ref[0].astype(F32))
 
     def cross(which, src, dst):
-        def body(t, _):
-            d = lax.rem(me + t, PEERS)
+        for dy, dx in AWAY:
             pltpu.make_async_remote_copy(
                 src_ref=src, dst_ref=dst.at[me],
                 send_sem=red_send.at[which], recv_sem=red.at[which],
-                device_id={"dap": d}, device_id_type=MESH,
+                device_id={"dap": peer(dy, dx)}, device_id_type=MESH,
             ).start()
-            return 0
-
-        lax.fori_loop(1, PEERS, body, 0)
         dst[me] = src[...]
 
     def all_gather(which, src, dst, rows):
         place = pl.ds(pl.multiple_of(my_dp * rows, 16), rows)
 
-        def body(t, _):
-            q = lax.rem(my_dp + t, ndp)
+        for dz, dr in crops:
             pltpu.make_async_remote_copy(
                 src_ref=src, dst_ref=dst.at[place],
                 send_sem=red_send.at[which], recv_sem=red.at[which],
-                device_id={"dp": q}, device_id_type=MESH,
+                device_id={"dp": crop(dz, dr)}, device_id_type=MESH,
             ).start()
-            return 0
-
-        lax.fori_loop(1, ndp, body, 0)
         dst[place, :] = src[...]
 
     rows_e, rows_f = EARLY // ndp, LATE // ndp
@@ -397,6 +428,13 @@
 
     lax.fori_loop(0, PIECES, lower, 0)
 
+    def put(n, src, dst):
+        copy = pltpu.make_async_copy(src, dst, out_sem.at[n])
+        copy.start()
+        return copy
+
+    puts = [put(0, out_grad, out_grad_h)]
+
     for m in range(4):
         m_at = slice(m * C, (m + 1) * C)
         g_f[m_at, :] = dot_nt(lnT[...], d_stack[m_at, :]).astype(BF16)
@@ -422,6 +460,7 @@
         mid_sum = mid_sum + block.astype(F32) * w_up[:, f_at].astype(F32)
     out_down[...] = ag_e[512:1024, :]
     out_out[...] = ag_e[1024:1280, :]
+    puts += [put(1, out_up, out_up_h), put(2, out_down, out_down_h), put(3, out_out, out_out_h)]
     pair_sum = ag_e[1024:1152, :].astype(F32) * w_out[0].astype(F32)
     tri_sum = ag_e[1152:1280, :].astype(F32) * w_out[1].astype(F32)
 
@@ -432,7 +471,10 @@
     out_proj[...] = ag_f[...]
     sums = [jnp.sum(s.T, axis=0, keepdims=True) for s in (pair_sum, tri_sum, mid_sum)]
     out_gains[...] = (jnp.concatenate(sums, axis=0) / gains[...]).astype(BF16)
-
+    puts += [put(4, out_proj, out_proj_h), put(5, out_gains, out_gains_h)]
+
+    for copy in puts:
+        copy.wait()
     for which, src in enumerate((s_l, s_r, s_t, s_d, s_dl, s_dr)):
         sent(which, src)
     sent_cot = r_c.at[pl.ds(0, PEERS - 1)]
@@ -449,10 +491,36 @@
     wait_count(ag_f.at[pl.ds(0, (ndp - 1) * rows_f)], red_send.at[5])
 
 
+def hand_over(outs, results):
+    count = len(outs)
+
+    def copies(*refs):
+        held = refs[2 * count:3 * count]
+        sems = refs[3 * count]
+        takes = [pltpu.make_async_copy(refs[n], held[n], sems.at[0, n]) for n in range(count)]
+        gives = [pltpu.make_async_copy(held[n], refs[count + n], sems.at[1, n]) for n in range(count)]
+        for take in takes:
+            take.start()
+        for take, give in zip(takes, gives):
+            take.wait()
+            give.start()
+        for give in gives:
+            give.wait()
+
+    hbm = pl.BlockSpec(memory_space=pl.ANY)
+    return pl.pallas_call(
+        copies,
+        out_shape=outs,
+        in_specs=[hbm] * count,
+        out_specs=(hbm,) * count,
+        scratch_shapes=[pltpu.VMEM(out.shape, BF16) for out in outs] + [pltpu.SemaphoreType.DMA((2, count))],
+        compiler_params=pltpu.CompilerParams(vmem_limit_bytes=63 * 1024 * 1024),
+        cost_estimate=pl.CostEstimate(flops=0, bytes_accessed=2_000_000, transcendentals=0),
+    )(*results)
+
+
 def local(ndp, pair_repr, cotangent, residue_mask, norm_gains, w_proj, w_out, w_up, w_down):
     scale = 1.0 / math.sqrt(ndp * C * C)
-    vmem = pl.BlockSpec(memory_space=pltpu.VMEM)
-    smem = pl.BlockSpec(memory_space=pltpu.SMEM)
     hbm = pl.BlockSpec(memory_space=pl.ANY)
     columns = ROWS * C
     chunks = pltpu.VMEM((PIECES, PEERS, PACK, C), BF16)
@@ -462,6 +530,13 @@
     cube = pltpu.VMEM((1024, C), F32)
     rows_e, rows_f = EARLY // ndp, LATE // ndp
     scratch = [
+        pltpu.VMEM((1024, C), BF16), pltpu.VMEM((1, C), jnp.int32), pltpu.VMEM((3, C), F32),
+        pltpu.VMEM((4, C, C), BF16), pltpu.VMEM((2, C, C), BF16),
+        pltpu.VMEM((C, FFN), BF16), pltpu.VMEM((FFN, C), BF16),
+        pltpu.VMEM((1024, C), BF16), pltpu.VMEM((4 * C, C), BF16), pltpu.VMEM((2 * C, C), BF16),
+        pltpu.VMEM((C, FFN), BF16), pltpu.VMEM((FFN, C), BF16), pltpu.VMEM((3, C), BF16),
+        pltpu.SemaphoreType.DMA((7,)), pltpu.SemaphoreType.DMA((6,)),
+        pltpu.VMEM((C, C), F32),
         pltpu.VMEM((3, C, C), F32),
         pltpu.VMEM((4 * C, C), BF16),
         pltpu.VMEM((2, C, C), BF16),
@@ -491,28 +566,24 @@
         pltpu.SemaphoreType.DMA((6,)),
         pltpu.SemaphoreType.DMA((6,)),
     ]
+    outs = tuple(
+        jax.ShapeDtypeStruct(shape, BF16)
+        for shape in ((1024, C), (1024, C), (4 * C, C), (2 * C, C), (C, FFN), (FFN, C), (3, C))
+    )
     results = pl.pallas_call(
         functools.partial(kernel, ndp, scale),
-        out_shape=(
-            jax.ShapeDtypeStruct((1024, C), BF16),
-            jax.ShapeDtypeStruct((1024, C), BF16),
-            jax.ShapeDtypeStruct((4 * C, C), BF16),
-            jax.ShapeDtypeStruct((2 * C, C), BF16),
-            jax.ShapeDtypeStruct((C, FFN), BF16),
-            jax.ShapeDtypeStruct((FFN, C), BF16),
-            jax.ShapeDtypeStruct((3, C), BF16),
-        ),
-        in_specs=[vmem, hbm, smem, vmem, vmem, vmem, vmem, vmem, vmem],
-        out_specs=(hbm, vmem, vmem, vmem, vmem, vmem, vmem),
+        out_shape=outs,
+        in_specs=[hbm] * 8,
+        out_specs=(hbm,) * 7,
         scratch_shapes=scratch,
         compiler_params=pltpu.CompilerParams(
-            collective_id=0, has_side_effects=True, vmem_limit_bytes=48 * 1024 * 1024
+            collective_id=0, has_side_effects=True, vmem_limit_bytes=63 * 1024 * 1024
         ),
         cost_estimate=pl.CostEstimate(flops=1_600_000_000, bytes_accessed=3_000_000, transcendentals=1_200_000),
     )(
-        pair_repr.reshape(1024, C), cotangent.reshape(1024, C), residue_mask, residue_mask,
-        norm_gains, w_proj, w_out, w_up, w_down,
+        pair_repr.reshape(1024, C), cotangent.reshape(1024, C), residue_mask, norm_gains, w_proj, w_out, w_up, w_down,
     )
+    results = hand_over(outs, results)
     nxt, grad, g_proj, g_out, g_up, g_down, g_gains = results
     return (
         nxt.reshape(1, C, ROWS, C),

time: 109 us -> 90.8 us (0.83)
  local copies, waits for them, and re-layouts: 10.7 us -> 0 us
  Pallas kernels: 97.4 us -> 90 us
    unnamed x23 -> x0, local copies, waits for them, and re-layouts: 10.7 us -> none
    pallas_call x1 -> x2, Pallas kernels: 97.4 us -> 90 us  [the longest x1 88 us: local(): pl.pallas_call(functools.partial(kernel, ndp, scale), out_shape=outs, in_...]
where the time goes in v2:
time: 90.8 us; the launch traced here: 90.7 us
  Pallas kernels  90 us (99%)
    pallas_call x1, Pallas kernels, local(): pl.pallas_call(functools.partial(kernel, ndp, scale), out_shape=outs, in_...  88 us
    pallas_call x1, Pallas kernels, hand_over(): pl.pallas_call(copies, out_shape=outs, in_specs=[hbm] * count, out_specs=...  2.01 us

profile of v2, /device:TPU:1, one launch (start us, length us, event | category | flops | bytes accessed | tf_op | source)
XLA Modules:
  0.0 90.7 jit_solution(11311543782047036667)
XLA Ops:
  0.6 88.0 %shard_map.135 = (bf16[1024,128]{1,0:T(8,128)(2,1)}, bf16[1024,128]{1,0:T(8,128)(2,1)}, bf16[512,128]{1,0:T(8,128)(2,1)}, bf16[256,128]{1,0:T(8,128)(2,1)}, bf16...) custom-call(bf16[1024,128]{1,0:T(8,128)(2,1)} %bitcast.6, bf16[1024,128]{1,0:T(8,128)(2,1)} %bitcast.7, ...), custom_call_target="tpu_custom_call" | custom-call | flops 1600000000 | bytes 3000000 | tf_op jit(solution)/shard_map/pallas_call | solution.py:573
  88.7 2.0 %shard_map.136 = (bf16[1024,128]{1,0:T(8,128)(2,1)}, bf16[1024,128]{1,0:T(8,128)(2,1)}, bf16[512,128]{1,0:T(8,128)(2,1)}, bf16[256,128]{1,0:T(8,128)(2,1)}, bf16...) custom-call(bf16[1024,128]{1,0:T(8,128)(2,1)} %get-tuple-element.21.refs_0_, ...), custom_call_target="tpu_custom_call" | custom-call | bytes 2000000 | tf_op jit(solution)/shard_map/pallas_call | solution.py:511

commit v3 on v2

--- a/solution.py
+++ b/solution.py
@@ -23,6 +23,7 @@
 PER = ROWS // PIECES
 WIDE = PER * C
 PACK = PER * 8
+PART = PEERS * PER
 EARLY = 1536
 LATE = 512
 
@@ -88,8 +89,8 @@
     mask_b, gain_b, wpT, woT, wuT, wdT, wcat,
     pairT, lnT, hat0, rstd0, ag, av, bg, bv,
     s_l, r_l, s_r, r_r, s_t, r_t, s_d, r_d, s_dl, r_dl, s_dr, r_dr, s_n, r_c,
-    x_l, x_r, lc, rc, y_l, y_r,
-    tri_ln, hid, mid_ln, d_pre, d_mid, d_stack, d_val, cotT,
+    x_p, y_p, x_r, y_r, lc, rc, dc,
+    tri_ln, hid, mid_b, mid_ln, d_pre, d_mid, d_stack, d_val, cotT,
     g_e, rs_e, ch_e, ex_e, fin_e, ag_e, g_f, rs_f, ch_f, ex_f, fin_f, ag_f,
     send, recv, once, once_send, red, red_send,
 ):
@@ -188,19 +189,20 @@
         bv[:, at] = value
         s_r[p] = split_rows(mask * gate * value).astype(BF16)
 
-    def front_send(p):
+    def front_step(p, _):
+        exchange(1, s_r, r_r, p)
+        front(p + 1)
+        return 0
+
+    def send_l(p, _):
         exchange(0, s_l, r_l, p)
-        exchange(1, s_r, r_r, p)
-
-    def front_step(p, _):
-        front_send(p)
-        front(p + 1)
         return 0
 
     front(0)
     pl.semaphore_wait(barrier, PEERS - 1 + ndp - 1)
     lax.fori_loop(0, PIECES - 1, front_step, 0)
-    front_send(PIECES - 1)
+    exchange(1, s_r, r_r, PIECES - 1)
+    lax.fori_loop(0, PIECES, send_l, 0)
 
     for dy, dx in AWAY:
         d = peer(dy, dx)
@@ -232,31 +234,30 @@
             [ref[pl.ds(pl.multiple_of(s * 64 + p * PACK, PACK), PACK), :] for s in range(PEERS)]
         ).astype(BF16)
 
-    def take_l(p, _):
-        arrived(0, r_l, p)
-        spread(x_l, r_l, p)
+    def take_r(p, _):
         arrived(1, r_r, p)
         spread(x_r, r_r, p)
         return 0
 
-    lax.fori_loop(0, PIECES, take_l, 0)
-
-    def tri_body(c, _):
-        left = x_l[pl.ds(c, C, 8), :].astype(BF16)
-        right = x_r[pl.ds(c, C, 8), :].astype(BF16)
-        lc[c] = left
-        rc[c] = right
-        y_l[pl.ds(c, C, 8), :] = dot_nt(left, right)
-        return 0
-
-    lax.fori_loop(0, 8, tri_body, 0)
-
-    def tri_send(p, _):
-        s_t[p] = gather_chunks(p)(y_l)
+    lax.fori_loop(0, PIECES, take_r, 0)
+    for c in range(8):
+        rc[c] = x_r[pl.ds(c, C, 8), :].astype(BF16)
+
+    def part(p):
+        return pl.ds(pl.multiple_of(p * PART, PART), PART)
+
+    def tri_step(p, _):
+        arrived(0, r_l, p)
+        x_p[...] = r_l[p].astype(F32).reshape(PEERS * PACK, C)
+        for c in range(8):
+            left = x_p[pl.ds(c, PART, 8), :].astype(BF16)
+            lc[c, part(p), :] = left
+            y_p[pl.ds(c, PART, 8), :] = dot_nt(left, rc[c])
+        s_t[p] = y_p[...].reshape(PEERS, PACK, C).astype(BF16)
         exchange(2, s_t, r_t, p)
         return 0
 
-    lax.fori_loop(0, PIECES, tri_send, 0)
+    lax.fori_loop(0, PIECES, tri_step, 0)
 
     own_cot.wait()
     all_cot = r_c.at[pl.ds(0, PEERS - 1)]
@@ -283,7 +284,9 @@
         tri_ln[:, at] = t_ln
         out_gate = jax.nn.sigmoid(dot(woT[0], lnT[:, at]))
         out_value = dot(woT[1], t_ln)
-        mid = (pairT[:, at] + out_gate * out_value).astype(BF16).astype(F32)
+        mid_r = (pairT[:, at] + out_gate * out_value).astype(BF16)
+        mid_b[:, at] = mid_r
+        mid = mid_r.astype(F32)
         mid_hat, mid_rstd = norm(mid)
         m_ln = (mid_hat * wide(gain_b[2])).astype(BF16)
         mid_ln[:, at] = m_ln
@@ -312,20 +315,19 @@
         d_tri = norm_back(dot(w_out[1], d_value), tri_hat, tri_rstd, wide(gain_b[1]))
         s_d[p] = split_rows(d_tri).astype(BF16)
         exchange(3, s_d, r_d, p)
-        nxt = mid + dot(wdT[...], hid[:, at])
+        return 0
+
+    lax.fori_loop(0, PIECES, middle, 0)
+
+    def send_next(p, _):
+        at = columns(p)
+        nxt = mid_b[:, at].astype(F32) + dot(wdT[...], hid[:, at])
         nxt_rows = jnp.concatenate(
             [nxt[:, r * C:(r + 1) * C].T.reshape(PEERS, 8, C) for r in range(PER)], axis=1
         )
         s_n[p] = nxt_rows.astype(BF16)
-        return 0
-
-    lax.fori_loop(0, PIECES, middle, 0)
-
-    def send_next(p, _):
         next_body(p)
         return 0
-
-    lax.fori_loop(0, PIECES, send_next, 0)
 
     def reduce_scatter(which, src, dst, rows):
         for dz, dr in crops:
@@ -376,49 +378,72 @@
     g_e[1152:1280, :] = dot_nt(tri_ln[...], d_val[...]).astype(BF16)
     reduce_scatter(0, g_e, rs_e, rows_e)
 
-    def take_d(p, _):
+    def back_step(p, _):
         arrived(3, r_d, p)
-        spread(x_l, r_d, p)
-        return 0
-
-    lax.fori_loop(0, PIECES, take_d, 0)
-
-    def back_body(c, _):
-        grad = x_l[pl.ds(c, C, 8), :].astype(BF16)
-        y_l[pl.ds(c, C, 8), :] = dot(grad, rc[c])
-        y_r[pl.ds(c, C, 8), :] = dot_tn(grad, lc[c])
-        return 0
-
-    lax.fori_loop(0, 8, back_body, 0)
-
-    def back_send(p, _):
-        s_dl[p] = gather_chunks(p)(y_l)
+        x_p[...] = r_d[p].astype(F32).reshape(PEERS * PACK, C)
+        for c in range(8):
+            grad = x_p[pl.ds(c, PART, 8), :].astype(BF16)
+            dc[c, part(p), :] = grad
+            y_p[pl.ds(c, PART, 8), :] = dot(grad, rc[c])
+        s_dl[p] = y_p[...].reshape(PEERS, PACK, C).astype(BF16)
         exchange(4, s_dl, r_dl, p)
+        return 0
+
+    lax.fori_loop(0, PIECES, back_step, 0)
+
+    for c in range(8):
+        y_r[pl.ds(c, C, 8), :] = dot_tn(dc[c], lc[c])
+
+    def back_right(p, _):
         s_dr[p] = gather_chunks(p)(y_r)
         exchange(5, s_dr, r_dr, p)
         return 0
 
-    lax.fori_loop(0, PIECES, back_send, 0)
+    lax.fori_loop(0, PIECES, back_right, 0)
+    lax.fori_loop(0, PIECES, send_next, 0)
 
     wait_count(rs_e.at[pl.ds(0, ndp - 1)], red.at[0])
     ch_e[...] = total(rs_e, ndp).astype(BF16)
     cross(1, ch_e, ex_e)
 
-    def lower(p, _):
+    def lower_left(p, _):
         at = columns(p)
-        mask = mask_of(p)
         arrived(4, r_dl, p)
-        grad = join_rows(r_dl[p].astype(F32)) * mask
+        grad = join_rows(r_dl[p].astype(F32)) * mask_of(p)
         gate = ag[:, at]
         with_gate = grad * gate
         d_stack[0:C, at] = (with_gate * av[:, at] * (1.0 - gate)).astype(BF16)
         d_stack[C:2 * C, at] = with_gate.astype(BF16)
+        return 0
+
+    def lower_right(p, _):
+        at = columns(p)
         arrived(5, r_dr, p)
-        grad = join_rows(r_dr[p].astype(F32)) * mask
+        grad = join_rows(r_dr[p].astype(F32)) * mask_of(p)
         gate = bg[:, at]
         with_gate = grad * gate
         d_stack[2 * C:3 * C, at] = (with_gate * bv[:, at] * (1.0 - gate)).astype(BF16)
         d_stack[3 * C:4 * C, at] = with_gate.astype(BF16)
+        return 0
+
+    def late_grads(first):
+        for m in (first, first + 1):
+            m_at = slice(m * C, (m + 1) * C)
+            g_f[m_at, :] = dot_nt(lnT[...], d_stack[m_at, :]).astype(BF16)
+
+    lax.fori_loop(0, PIECES, lower_left, 0)
+    late_grads(0)
+    lax.fori_loop(0, PIECES, lower_right, 0)
+    late_grads(2)
+    reduce_scatter(2, g_f, rs_f, rows_f)
+
+    def put(n, src, dst):
+        copy = pltpu.make_async_copy(src, dst, out_sem.at[n])
+        copy.start()
+        return copy
+
+    def finish(p, _):
+        at = columns(p)
         d_ln = dot(wcat[...], d_stack[:, at])
         result = d_mid[:, at] + norm_back(d_ln, hat0[:, at], rstd0[:, at], wide(gain_b[0]))
         for r in range(PER):
@@ -426,19 +451,8 @@
             out_grad[row, :] = result[:, r * C:(r + 1) * C].T.astype(BF16)
         return 0
 
-    lax.fori_loop(0, PIECES, lower, 0)
-
-    def put(n, src, dst):
-        copy = pltpu.make_async_copy(src, dst, out_sem.at[n])
-        copy.start()
-        return copy
-
+    lax.fori_loop(0, PIECES, finish, 0)
     puts = [put(0, out_grad, out_grad_h)]
-
-    for m in range(4):
-        m_at = slice(m * C, (m + 1) * C)
-        g_f[m_at, :] = dot_nt(lnT[...], d_stack[m_at, :]).astype(BF16)
-    reduce_scatter(2, g_f, rs_f, rows_f)
 
     wait_count(ex_e.at[pl.ds(0, PEERS - 1)], red.at[1])
     fin_e[...] = (total(ex_e, PEERS) * scale).astype(BF16)
@@ -546,8 +560,9 @@
         full, half, full, pltpu.VMEM((1, columns), F32), full, full, full, full,
         *([chunks] * 13),
         pltpu.VMEM((PEERS, 64, C), BF16),
-        cube, cube, pltpu.VMEM((8, C, C), BF16), pltpu.VMEM((8, C, C), BF16), cube, cube,
-        half, big, half, big, full, pltpu.VMEM((5 * C, columns), BF16), half, half,
+        pltpu.VMEM((PEERS * PACK, C), F32), pltpu.VMEM((PEERS * PACK, C), F32), cube, cube,
+        *([pltpu.VMEM((8, C, C), BF16)] * 3),
+        half, big, half, half, big, full, pltpu.VMEM((5 * C, columns), BF16), half, half,
     ]
     for rows, whole in ((rows_e, EARLY), (rows_f, LATE)):
         scratch += [

time: 90.8 us -> 84.9 us (0.935)
  Pallas kernels: 90 us -> 84.1 us
    pallas_call x1, Pallas kernels: 88 us -> 82.1 us  [local(): pl.pallas_call(functools.partial(kernel, ndp, scale), out_shape=outs, in_...]
where the time goes in v3:
time: 84.9 us; the launch traced here: 84.7 us
  Pallas kernels  84.1 us (99%)
    pallas_call x1, Pallas kernels, local(): pl.pallas_call(functools.partial(kernel, ndp, scale), out_shape=outs, in_...  82.1 us
    pallas_call x1, Pallas kernels, hand_over(): pl.pallas_call(copies, out_shape=outs, in_specs=[hbm] * count, out_specs=...  2.01 us

profile of v3, /device:TPU:1, one launch (start us, length us, event | category | flops | bytes accessed | tf_op | source)
XLA Modules:
  0.0 84.7 jit_solution(8123051861589457997)
XLA Ops:
  0.6 82.1 %shard_map.135 = (bf16[1024,128]{1,0:T(8,128)(2,1)}, bf16[1024,128]{1,0:T(8,128)(2,1)}, bf16[512,128]{1,0:T(8,128)(2,1)}, bf16[256,128]{1,0:T(8,128)(2,1)}, bf16...) custom-call(bf16[1024,128]{1,0:T(8,128)(2,1)} %bitcast.6, bf16[1024,128]{1,0:T(8,128)(2,1)} %bitcast.7, ...), custom_call_target="tpu_custom_call" | custom-call | flops 1600000000 | bytes 3000000 | tf_op jit(solution)/shard_map/pallas_call | solution.py:588
  82.7 2.0 %shard_map.136 = (bf16[1024,128]{1,0:T(8,128)(2,1)}, bf16[1024,128]{1,0:T(8,128)(2,1)}, bf16[512,128]{1,0:T(8,128)(2,1)}, bf16[256,128]{1,0:T(8,128)(2,1)}, bf16...) custom-call(bf16[1024,128]{1,0:T(8,128)(2,1)} %get-tuple-element.21.refs_0_, ...), custom_call_target="tpu_custom_call" | custom-call | bytes 2000000 | tf_op jit(solution)/shard_map/pallas_call | solution.py:525

commit v4 on v3

--- a/solution.py
+++ b/solution.py
@@ -83,15 +83,14 @@
 def kernel(
     ndp, scale,
     pair_h, cot, mask_h, gains_h, w_proj_h, w_out_h, w_up_h, w_down_h,
-    out_next, out_grad_h, out_proj_h, out_out_h, out_up_h, out_down_h, out_gains_h,
-    pair, mask_v, gains, w_proj, w_out, w_up, w_down,
-    out_grad, out_proj, out_out, out_up, out_down, out_gains, in_sem, out_sem,
+    out_next, out_grad, out_proj, out_out, out_up, out_down, out_gains,
+    pair, mask_v, gains, w_proj, w_out, w_up, w_down, in_sem,
     mask_b, gain_b, wpT, woT, wuT, wdT, wcat,
     pairT, lnT, hat0, rstd0, ag, av, bg, bv,
     s_l, r_l, s_r, r_r, s_t, r_t, s_d, r_d, s_dl, r_dl, s_dr, r_dr, s_n, r_c,
     x_p, y_p, x_r, y_r, lc, rc, dc,
     tri_ln, hid, mid_b, mid_ln, d_pre, d_mid, d_stack, d_val, cotT,
-    g_e, rs_e, ch_e, ex_e, fin_e, ag_e, g_f, rs_f, ch_f, ex_f, fin_f, ag_f,
+    g_e, sib_e, half_e, rs_e, ch_e, ex_e, fin_e, ag_e, g_f, rs_f, ch_f, ex_f, fin_f, ag_f,
     send, recv, once, once_send, red, red_send,
 ):
     me = lax.axis_index("dap")
@@ -204,15 +203,18 @@
     exchange(1, s_r, r_r, PIECES - 1)
     lax.fori_loop(0, PIECES, send_l, 0)
 
-    for dy, dx in AWAY:
-        d = peer(dy, dx)
-        pltpu.make_async_remote_copy(
-            src_ref=cot.at[pl.ds(pl.multiple_of(d * 64, 64), 64)], dst_ref=r_c.at[me],
-            send_sem=once_send.at[0], recv_sem=once.at[0],
-            device_id={"dap": d}, device_id_type=MESH,
-        ).start()
-    own_cot = pltpu.make_async_copy(cot.at[pl.ds(pl.multiple_of(me * 64, 64), 64)], r_c.at[me], once.at[1])
+    own_cot = pltpu.make_async_copy(cot.at[pl.ds(pl.multiple_of(me * 64, 64), 64)], r_c.at[me], once.at[0])
     own_cot.start()
+
+    def send_cot(p):
+        here = pl.ds(pl.multiple_of(p * PACK, PACK), PACK)
+        for dy, dx in AWAY:
+            d = peer(dy, dx)
+            pltpu.make_async_remote_copy(
+                src_ref=cot.at[pl.ds(pl.multiple_of(d * 64 + p * PACK, PACK), PACK)], dst_ref=r_c.at[me, here],
+                send_sem=once_send.at[0], recv_sem=recv.at[6, p],
+                device_id={"dap": d}, device_id_type=MESH,
+            ).start()
 
     for load in loads[4:]:
         load.wait()
@@ -255,13 +257,12 @@
             y_p[pl.ds(c, PART, 8), :] = dot_nt(left, rc[c])
         s_t[p] = y_p[...].reshape(PEERS, PACK, C).astype(BF16)
         exchange(2, s_t, r_t, p)
+        send_cot(p)
         return 0
 
     lax.fori_loop(0, PIECES, tri_step, 0)
 
     own_cot.wait()
-    all_cot = r_c.at[pl.ds(0, PEERS - 1)]
-    pltpu.make_async_copy(all_cot, all_cot, once.at[0]).wait()
 
     def next_body(p):
         rows = pl.ds(pl.multiple_of(me * 64 + p * PACK, PACK), PACK)
@@ -290,6 +291,8 @@
         mid_hat, mid_rstd = norm(mid)
         m_ln = (mid_hat * wide(gain_b[2])).astype(BF16)
         mid_ln[:, at] = m_ln
+        cot_piece = r_c.at[pl.ds(0, PEERS - 1), pl.ds(0, PACK)]
+        pltpu.make_async_copy(cot_piece, cot_piece, recv.at[6, p]).wait()
         cot_rows = r_c[:, pl.ds(pl.multiple_of(p * PACK, PACK), PACK), :].astype(F32)
         cot_t = jnp.concatenate(
             [cot_rows[:, r * 8:(r + 1) * 8, :].reshape(C, C).T for r in range(PER)], axis=1
@@ -329,24 +332,70 @@
         next_body(p)
         return 0
 
-    def reduce_scatter(which, src, dst, rows):
-        for dz, dr in crops:
-            q = crop(dz, dr)
-            pltpu.make_async_remote_copy(
-                src_ref=src.at[pl.ds(pl.multiple_of(q * rows, 16), rows)], dst_ref=dst.at[my_dp],
-                send_sem=red_send.at[which], recv_sem=red.at[which],
-                device_id={"dp": q}, device_id_type=MESH,
-            ).start()
-        dst[my_dp] = src[pl.ds(pl.multiple_of(my_dp * rows, 16), rows), :]
+    rows_e, rows_f = EARLY // ndp, LATE // ndp
+
+    core = lax.rem(my_dp, 2)
+    place_dp = my_dp // 2
+    places = ndp // 2
+    sibling = {"dp": place_dp * 2 + 1 - core}
+    half_rows = EARLY // 2
+
+    def core_half(which):
+        return pl.ds(pl.multiple_of(which * half_rows, 16), half_rows)
+
+    chips = [(dz, dr) for dz, dr in crops if dr % 2 == 0]
+
+    def chip(dz, dr):
+        return crop(dz, dr) // 2
+
+    def spread_early():
+        for dz, dr in chips:
+            q = chip(dz, dr)
+            pltpu.make_async_remote_copy(
+                src_ref=half_e.at[pl.ds(pl.multiple_of(q * rows_e, 16), rows_e)], dst_ref=rs_e.at[place_dp],
+                send_sem=red_send.at[0], recv_sem=red.at[0],
+                device_id={"dp": q * 2 + core}, device_id_type=MESH,
+            ).start()
+        rs_e[place_dp] = half_e[pl.ds(pl.multiple_of(place_dp * rows_e, 16), rows_e), :]
+
+    def gather_early():
+        place = pl.ds(pl.multiple_of(core * half_rows + place_dp * rows_e, 16), rows_e)
+        for dz, dr in chips:
+            pltpu.make_async_remote_copy(
+                src_ref=fin_e, dst_ref=ag_e.at[place],
+                send_sem=red_send.at[4], recv_sem=red.at[4],
+                device_id={"dp": chip(dz, dr) * 2 + core}, device_id_type=MESH,
+            ).start()
+        ag_e[place, :] = fin_e[...]
+
+    def spread_late(side):
+        target = 1 - side
+        for dz, dr in chips:
+            q = chip(dz, dr)
+            pltpu.make_async_remote_copy(
+                src_ref=g_f.at[pl.ds(pl.multiple_of(side * 2 * C + q * rows_f, 16), rows_f)], dst_ref=rs_f.at[my_dp],
+                send_sem=red_send.at[2], recv_sem=red.at[2],
+                device_id={"dp": q * 2 + target}, device_id_type=MESH,
+            ).start()
+        own = pl.ds(pl.multiple_of(side * 2 * C + place_dp * rows_f, 16), rows_f)
+
+        @pl.when(core == target)
+        def _():
+            rs_f[my_dp] = g_f[own, :]
+
+        @pl.when(core != target)
+        def _():
+            pltpu.make_async_remote_copy(
+                src_ref=g_f.at[own], dst_ref=rs_f.at[my_dp],
+                send_sem=red_send.at[2], recv_sem=red.at[2],
+                device_id=sibling, device_id_type=MESH,
+            ).start()
 
     def wait_count(ref, sem):
         pltpu.make_async_copy(ref, ref, sem).wait()
 
-    def total(ref, count):
-        def body(n, value):
-            return value + ref[n].astype(F32)
-
-        return lax.fori_loop(1, count, body, ref[0].astype(F32))
+    def total(ref):
+        return jnp.sum(ref[...].astype(F32), axis=0)
 
     def cross(which, src, dst):
         for dy, dx in AWAY:
@@ -357,8 +406,8 @@
             ).start()
         dst[me] = src[...]
 
-    def all_gather(which, src, dst, rows):
-        place = pl.ds(pl.multiple_of(my_dp * rows, 16), rows)
+    def gather_late(which, src, dst, rows):
+        place = pl.ds(pl.multiple_of((1 - core) * 2 * C + place_dp * rows, 16), rows)
 
         for dz, dr in crops:
             pltpu.make_async_remote_copy(
@@ -367,8 +416,6 @@
                 device_id={"dp": crop(dz, dr)}, device_id_type=MESH,
             ).start()
         dst[place, :] = src[...]
-
-    rows_e, rows_f = EARLY // ndp, LATE // ndp
 
     for f in range(4):
         f_at = slice(f * C, (f + 1) * C)
@@ -376,7 +423,12 @@
         g_e[512 + f * C:512 + (f + 1) * C, :] = dot_nt(hid[f_at, :], cotT[...]).astype(BF16)
     g_e[1024:1152, :] = dot_nt(lnT[...], d_stack[4 * C:5 * C, :]).astype(BF16)
     g_e[1152:1280, :] = dot_nt(tri_ln[...], d_val[...]).astype(BF16)
-    reduce_scatter(0, g_e, rs_e, rows_e)
+    add_cores = pltpu.make_async_remote_copy(
+        src_ref=g_e.at[core_half(1 - core)], dst_ref=sib_e,
+        send_sem=red_send.at[1], recv_sem=red.at[6],
+        device_id=sibling, device_id_type=MESH,
+    )
+    add_cores.start()
 
     def back_step(p, _):
         arrived(3, r_d, p)
@@ -389,7 +441,11 @@
         exchange(4, s_dl, r_dl, p)
         return 0
 
-    lax.fori_loop(0, PIECES, back_step, 0)
+    back_step(0, 0)
+    add_cores.wait_recv()
+    half_e[...] = (g_e[core_half(core), :].astype(F32) + sib_e[...].astype(F32)).astype(BF16)
+    spread_early()
+    lax.fori_loop(1, PIECES, back_step, 0)
 
     for c in range(8):
         y_r[pl.ds(c, C, 8), :] = dot_tn(dc[c], lc[c])
@@ -401,10 +457,6 @@
 
     lax.fori_loop(0, PIECES, back_right, 0)
     lax.fori_loop(0, PIECES, send_next, 0)
-
-    wait_count(rs_e.at[pl.ds(0, ndp - 1)], red.at[0])
-    ch_e[...] = total(rs_e, ndp).astype(BF16)
-    cross(1, ch_e, ex_e)
 
     def lower_left(p, _):
         at = columns(p)
@@ -433,14 +485,13 @@
 
     lax.fori_loop(0, PIECES, lower_left, 0)
     late_grads(0)
+    spread_late(0)
+    wait_count(rs_e.at[pl.ds(0, places - 1)], red.at[0])
+    ch_e[...] = total(rs_e).astype(BF16)
+    cross(5, ch_e, ex_e)
     lax.fori_loop(0, PIECES, lower_right, 0)
     late_grads(2)
-    reduce_scatter(2, g_f, rs_f, rows_f)
-
-    def put(n, src, dst):
-        copy = pltpu.make_async_copy(src, dst, out_sem.at[n])
-        copy.start()
-        return copy
+    spread_late(1)
 
     def finish(p, _):
         at = columns(p)
@@ -452,20 +503,26 @@
         return 0
 
     lax.fori_loop(0, PIECES, finish, 0)
-    puts = [put(0, out_grad, out_grad_h)]
-
-    wait_count(ex_e.at[pl.ds(0, PEERS - 1)], red.at[1])
-    fin_e[...] = (total(ex_e, PEERS) * scale).astype(BF16)
-    all_gather(4, fin_e, ag_e, rows_e)
+
+    wait_count(ex_e.at[pl.ds(0, PEERS - 1)], red.at[5])
+    fin_e[...] = (total(ex_e) * scale).astype(BF16)
+    gather_early()
 
     wait_count(rs_f.at[pl.ds(0, ndp - 1)], red.at[2])
-    ch_f[...] = total(rs_f, ndp).astype(BF16)
+    ch_f[...] = total(rs_f).astype(BF16)
     cross(3, ch_f, ex_f)
     wait_count(ex_f.at[pl.ds(0, PEERS - 1)], red.at[3])
-    fin_f[...] = (total(ex_f, PEERS) * scale).astype(BF16)
-    all_gather(5, fin_f, ag_f, rows_f)
-
-    wait_count(ag_e.at[pl.ds(0, (ndp - 1) * rows_e)], red.at[4])
+    fin_f[...] = (total(ex_f) * scale).astype(BF16)
+    gather_late(7, fin_f, ag_f, rows_f)
+
+    wait_count(ag_e.at[pl.ds(0, (places - 1) * rows_e)], red.at[4])
+    to_core = pltpu.make_async_remote_copy(
+        src_ref=ag_e.at[core_half(core)], dst_ref=ag_e.at[core_half(core)],
+        send_sem=red_send.at[6], recv_sem=red.at[1],
+        device_id=sibling, device_id_type=MESH,
+    )
+    to_core.start()
+    to_core.wait_recv()
     mid_sum = jnp.zeros((C, C), F32)
     for f in range(4):
         f_at = slice(f * C, (f + 1) * C)
@@ -474,21 +531,17 @@
         mid_sum = mid_sum + block.astype(F32) * w_up[:, f_at].astype(F32)
     out_down[...] = ag_e[512:1024, :]
     out_out[...] = ag_e[1024:1280, :]
-    puts += [put(1, out_up, out_up_h), put(2, out_down, out_down_h), put(3, out_out, out_out_h)]
     pair_sum = ag_e[1024:1152, :].astype(F32) * w_out[0].astype(F32)
     tri_sum = ag_e[1152:1280, :].astype(F32) * w_out[1].astype(F32)
 
-    wait_count(ag_f.at[pl.ds(0, (ndp - 1) * rows_f)], red.at[5])
+    wait_count(ag_f.at[pl.ds(0, (ndp - 1) * rows_f)], red.at[7])
     for m in range(4):
         block = ag_f[m * C:(m + 1) * C, :]
         pair_sum = pair_sum + block.astype(F32) * w_proj[m].astype(F32)
     out_proj[...] = ag_f[...]
     sums = [jnp.sum(s.T, axis=0, keepdims=True) for s in (pair_sum, tri_sum, mid_sum)]
     out_gains[...] = (jnp.concatenate(sums, axis=0) / gains[...]).astype(BF16)
-    puts += [put(4, out_proj, out_proj_h), put(5, out_gains, out_gains_h)]
-
-    for copy in puts:
-        copy.wait()
+
     for which, src in enumerate((s_l, s_r, s_t, s_d, s_dl, s_dr)):
         sent(which, src)
     sent_cot = r_c.at[pl.ds(0, PEERS - 1)]
@@ -497,45 +550,42 @@
     wait_count(all_next, once_send.at[1])
     wait_count(all_next, once.at[2])
     wait_count(s_n.at[:, 0], once.at[3])
-    wait_count(rs_e.at[pl.ds(0, ndp - 1)], red_send.at[0])
-    wait_count(ex_e.at[pl.ds(0, PEERS - 1)], red_send.at[1])
+    add_cores.wait_send()
+    to_core.wait_send()
+    wait_count(rs_e.at[pl.ds(0, places - 1)], red_send.at[0])
+    wait_count(ex_e.at[pl.ds(0, PEERS - 1)], red_send.at[5])
     wait_count(rs_f.at[pl.ds(0, ndp - 1)], red_send.at[2])
     wait_count(ex_f.at[pl.ds(0, PEERS - 1)], red_send.at[3])
-    wait_count(ag_e.at[pl.ds(0, (ndp - 1) * rows_e)], red_send.at[4])
-    wait_count(ag_f.at[pl.ds(0, (ndp - 1) * rows_f)], red_send.at[5])
+    wait_count(ag_e.at[pl.ds(0, (places - 1) * rows_e)], red_send.at[4])
+    wait_count(ag_f.at[pl.ds(0, (ndp - 1) * rows_f)], red_send.at[7])
 
 
 def hand_over(outs, results):
     count = len(outs)
 
     def copies(*refs):
-        held = refs[2 * count:3 * count]
-        sems = refs[3 * count]
-        takes = [pltpu.make_async_copy(refs[n], held[n], sems.at[0, n]) for n in range(count)]
-        gives = [pltpu.make_async_copy(held[n], refs[count + n], sems.at[1, n]) for n in range(count)]
-        for take in takes:
-            take.start()
-        for take, give in zip(takes, gives):
-            take.wait()
+        sems = refs[2 * count]
+        gives = [pltpu.make_async_copy(refs[n], refs[count + n], sems.at[n]) for n in range(count)]
+        for give in gives:
             give.start()
         for give in gives:
             give.wait()
 
-    hbm = pl.BlockSpec(memory_space=pl.ANY)
     return pl.pallas_call(
         copies,
         out_shape=outs,
-        in_specs=[hbm] * count,
-        out_specs=(hbm,) * count,
-        scratch_shapes=[pltpu.VMEM(out.shape, BF16) for out in outs] + [pltpu.SemaphoreType.DMA((2, count))],
-        compiler_params=pltpu.CompilerParams(vmem_limit_bytes=63 * 1024 * 1024),
+        in_specs=[pl.BlockSpec(memory_space=pltpu.VMEM)] * count,
+        out_specs=(pl.BlockSpec(memory_space=pltpu.HBM),) * count,
+        scratch_shapes=[pltpu.SemaphoreType.DMA((count,))],
+        compiler_params=pltpu.CompilerParams(vmem_limit_bytes=48 * 1024 * 1024),
         cost_estimate=pl.CostEstimate(flops=0, bytes_accessed=2_000_000, transcendentals=0),
     )(*results)
 
 
 def local(ndp, pair_repr, cotangent, residue_mask, norm_gains, w_proj, w_out, w_up, w_down):
     scale = 1.0 / math.sqrt(ndp * C * C)
-    hbm = pl.BlockSpec(memory_space=pl.ANY)
+    hbm = pl.BlockSpec(memory_space=pltpu.HBM)
+    vmem = pl.BlockSpec(memory_space=pltpu.VMEM)
     columns = ROWS * C
     chunks = pltpu.VMEM((PIECES, PEERS, PACK, C), BF16)
     full = pltpu.VMEM((C, columns), F32)
@@ -547,9 +597,7 @@
         pltpu.VMEM((1024, C), BF16), pltpu.VMEM((1, C), jnp.int32), pltpu.VMEM((3, C), F32),
         pltpu.VMEM((4, C, C), BF16), pltpu.VMEM((2, C, C), BF16),
         pltpu.VMEM((C, FFN), BF16), pltpu.VMEM((FFN, C), BF16),
-        pltpu.VMEM((1024, C), BF16), pltpu.VMEM((4 * C, C), BF16), pltpu.VMEM((2 * C, C), BF16),
-        pltpu.VMEM((C, FFN), BF16), pltpu.VMEM((FFN, C), BF16), pltpu.VMEM((3, C), BF16),
-        pltpu.SemaphoreType.DMA((7,)), pltpu.SemaphoreType.DMA((6,)),
+        pltpu.SemaphoreType.DMA((7,)),
         pltpu.VMEM((C, C), F32),
         pltpu.VMEM((3, C, C), F32),
         pltpu.VMEM((4 * C, C), BF16),
@@ -564,10 +612,16 @@
         *([pltpu.VMEM((8, C, C), BF16)] * 3),
         half, big, half, half, big, full, pltpu.VMEM((5 * C, columns), BF16), half, half,
     ]
+    scratch += [
+        pltpu.VMEM((EARLY, C), BF16),
+        pltpu.VMEM((EARLY // 2, C), BF16),
+        pltpu.VMEM((EARLY // 2, C), BF16),
+        pltpu.VMEM((ndp // 2, rows_e, C), BF16),
+    ]
     for rows, whole in ((rows_e, EARLY), (rows_f, LATE)):
+        if whole == LATE:
+            scratch += [pltpu.VMEM((whole, C), BF16), pltpu.VMEM((ndp, rows, C), BF16)]
         scratch += [
-            pltpu.VMEM((whole, C), BF16),
-            pltpu.VMEM((ndp, rows, C), BF16),
             pltpu.VMEM((rows, C), BF16),
             pltpu.VMEM((PEERS, rows, C), BF16),
             pltpu.VMEM((rows, C), BF16),
@@ -575,11 +629,11 @@
         ]
     scratch += [
         pltpu.SemaphoreType.DMA((6,)),
-        pltpu.SemaphoreType.DMA((6, PIECES)),
+        pltpu.SemaphoreType.DMA((7, PIECES)),
         pltpu.SemaphoreType.DMA((4,)),
         pltpu.SemaphoreType.DMA((2,)),
-        pltpu.SemaphoreType.DMA((6,)),
-        pltpu.SemaphoreType.DMA((6,)),
+        pltpu.SemaphoreType.DMA((8,)),
+        pltpu.SemaphoreType.DMA((8,)),
     ]
     outs = tuple(
         jax.ShapeDtypeStruct(shape, BF16)
@@ -589,14 +643,20 @@
         functools.partial(kernel, ndp, scale),
         out_shape=outs,
         in_specs=[hbm] * 8,
-        out_specs=(hbm,) * 7,
+        out_specs=(vmem,) * 7,
         scratch_shapes=scratch,
         compiler_params=pltpu.CompilerParams(
-            collective_id=0, has_side_effects=True, vmem_limit_bytes=63 * 1024 * 1024
+            collective_id=0, has_side_effects=True, vmem_limit_bytes=48 * 1024 * 1024
         ),
         cost_estimate=pl.CostEstimate(flops=1_600_000_000, bytes_accessed=3_000_000, transcendentals=1_200_000),
     )(
-        pair_repr.reshape(1024, C), cotangent.reshape(1024, C), residue_mask, norm_gains, w_proj, w_out, w_up, w_down,
+        *[
+            pltpu.with_memory_space_constraint(array, pltpu.HBM)
+            for array in (
+                pair_repr.reshape(1024, C), cotangent.reshape(1024, C), residue_mask, norm_gains,
+                w_proj, w_out, w_up, w_down,
+            )
+        ]
     )
     results = hand_over(outs, results)
     nxt, grad, g_proj, g_out, g_up, g_down, g_gains = results

time: 84.9 us -> 82.8 us (0.975)
  Pallas kernels: 84.1 us -> 82 us
    pallas_call x1, Pallas kernels: 82.1 us -> 81 us  [local(): pl.pallas_call(functools.partial(kernel, ndp, scale), out_shape=outs, in_...]
    pallas_call x1, Pallas kernels: 2.01 us -> 1 us  [hand_over(): pl.pallas_call(copies, out_shape=outs, in_specs=[pl.BlockSpec(memory_spac...]
where the time goes in v4:
time: 82.8 us; the launch traced here: 82.7 us
  Pallas kernels  82 us (99%)
    pallas_call x1, Pallas kernels, local(): pl.pallas_call(functools.partial(kernel, ndp, scale), out_shape=outs, in_...  81 us

profile of v4, /device:TPU:1, one launch (start us, length us, event | category | flops | bytes accessed | tf_op | source)
XLA Modules:
  0.0 82.7 jit_solution(12572566974748943986)
XLA Ops:
  0.6 81.0 %shard_map.135 = (bf16[1024,128]{1,0:T(8,128)(2,1)S(1)}, bf16[1024,128]{1,0:T(8,128)(2,1)S(1)}, bf16[512,128]{1,0:T(8,128)(2,1)S(1)}, bf16[256,128]{1,0:T(8,128)...) custom-call(bf16[1024,128]{1,0:T(8,128)(2,1)} %bitcast.6, ...), custom_call_target="tpu_custom_call" | custom-call | flops 1600000000 | bytes 3000000 | tf_op jit(solution)/shard_map/pallas_call | solution.py:642
  81.7 1.0 %shard_map.136 = (bf16[1024,128]{1,0:T(8,128)(2,1)}, bf16[1024,128]{1,0:T(8,128)(2,1)}, bf16[512,128]{1,0:T(8,128)(2,1)}, bf16[256,128]{1,0:T(8,128)(2,1)}, bf16...) custom-call(bf16[1024,128]{1,0:T(8,128)(2,1)S(1)} %get-tuple-element.21.refs_0_, ...), custom_call_target="tpu_custom_call" | custom-call | bytes 2000000 | tf_op jit(solution)/shard_map/pallas_call | solution.py:574

commit v5 on v4

--- a/solution.py
+++ b/solution.py
@@ -85,7 +85,7 @@
     pair_h, cot, mask_h, gains_h, w_proj_h, w_out_h, w_up_h, w_down_h,
     out_next, out_grad, out_proj, out_out, out_up, out_down, out_gains,
     pair, mask_v, gains, w_proj, w_out, w_up, w_down, in_sem,
-    mask_b, gain_b, wpT, woT, wuT, wdT, wcat,
+    held_g, mask_b, gain_b, wpT, woT, wuT, wdT, wcat,
     pairT, lnT, hat0, rstd0, ag, av, bg, bv,
     s_l, r_l, s_r, r_r, s_t, r_t, s_d, r_d, s_dl, r_dl, s_dr, r_dr, s_n, r_c,
     x_p, y_p, x_r, y_r, lc, rc, dc,
@@ -250,12 +250,12 @@
 
     def tri_step(p, _):
         arrived(0, r_l, p)
-        x_p[...] = r_l[p].astype(F32).reshape(PEERS * PACK, C)
+        x_p[0:PEERS * PACK, :] = r_l[p].astype(F32).reshape(PEERS * PACK, C)
         for c in range(8):
             left = x_p[pl.ds(c, PART, 8), :].astype(BF16)
             lc[c, part(p), :] = left
             y_p[pl.ds(c, PART, 8), :] = dot_nt(left, rc[c])
-        s_t[p] = y_p[...].reshape(PEERS, PACK, C).astype(BF16)
+        s_t[p] = y_p[0:PEERS * PACK, :].reshape(PEERS, PACK, C).astype(BF16)
         exchange(2, s_t, r_t, p)
         send_cot(p)
         return 0
@@ -264,7 +264,7 @@
 
     own_cot.wait()
 
-    def next_body(p):
+    def send_next(p, _):
         rows = pl.ds(pl.multiple_of(me * 64 + p * PACK, PACK), PACK)
 
         for dy, dx in AWAY:
@@ -275,6 +275,7 @@
                 device_id={"dap": d}, device_id_type=MESH,
             ).start()
         pltpu.make_async_copy(s_n.at[p, me], out_next.at[rows], once.at[3]).start()
+        return 0
 
     def middle(p, _):
         at = columns(p)
@@ -322,14 +323,13 @@
 
     lax.fori_loop(0, PIECES, middle, 0)
 
-    def send_next(p, _):
+    def make_next(p, _):
         at = columns(p)
         nxt = mid_b[:, at].astype(F32) + dot(wdT[...], hid[:, at])
         nxt_rows = jnp.concatenate(
             [nxt[:, r * C:(r + 1) * C].T.reshape(PEERS, 8, C) for r in range(PER)], axis=1
         )
         s_n[p] = nxt_rows.astype(BF16)
-        next_body(p)
         return 0
 
     rows_e, rows_f = EARLY // ndp, LATE // ndp
@@ -432,12 +432,12 @@
 
     def back_step(p, _):
         arrived(3, r_d, p)
-        x_p[...] = r_d[p].astype(F32).reshape(PEERS * PACK, C)
+        x_p[0:PEERS * PACK, :] = r_d[p].astype(F32).reshape(PEERS * PACK, C)
         for c in range(8):
             grad = x_p[pl.ds(c, PART, 8), :].astype(BF16)
             dc[c, part(p), :] = grad
             y_p[pl.ds(c, PART, 8), :] = dot(grad, rc[c])
-        s_dl[p] = y_p[...].reshape(PEERS, PACK, C).astype(BF16)
+        s_dl[p] = y_p[0:PEERS * PACK, :].reshape(PEERS, PACK, C).astype(BF16)
         exchange(4, s_dl, r_dl, p)
         return 0
 
@@ -456,7 +456,7 @@
         return 0
 
     lax.fori_loop(0, PIECES, back_right, 0)
-    lax.fori_loop(0, PIECES, send_next, 0)
+    lax.fori_loop(0, PIECES, make_next, 0)
 
     def lower_left(p, _):
         at = columns(p)
@@ -478,19 +478,22 @@
         d_stack[3 * C:4 * C, at] = with_gate.astype(BF16)
         return 0
 
-    def late_grads(first):
-        for m in (first, first + 1):
-            m_at = slice(m * C, (m + 1) * C)
-            g_f[m_at, :] = dot_nt(lnT[...], d_stack[m_at, :]).astype(BF16)
-
     lax.fori_loop(0, PIECES, lower_left, 0)
-    late_grads(0)
+    for m in (0, 1):
+        m_at = slice(m * C, (m + 1) * C)
+        g_f[m_at, :] = dot_nt(lnT[...], d_stack[m_at, :]).astype(BF16)
     spread_late(0)
     wait_count(rs_e.at[pl.ds(0, places - 1)], red.at[0])
     ch_e[...] = total(rs_e).astype(BF16)
     cross(5, ch_e, ex_e)
-    lax.fori_loop(0, PIECES, lower_right, 0)
-    late_grads(2)
+    head = (PIECES - 1) * WIDE
+    lax.fori_loop(0, PIECES - 1, lower_right, 0)
+    for m in (2, 3):
+        held_g[m - 2] = dot_nt(lnT[:, :head], d_stack[m * C:(m + 1) * C, :head])
+    lower_right(PIECES - 1, 0)
+    for m in (2, 3):
+        m_at = slice(m * C, (m + 1) * C)
+        g_f[m_at, :] = (held_g[m - 2] + dot_nt(lnT[:, head:], d_stack[m_at, head:])).astype(BF16)
     spread_late(1)
 
     def finish(p, _):
@@ -503,6 +506,7 @@
         return 0
 
     lax.fori_loop(0, PIECES, finish, 0)
+    lax.fori_loop(0, PIECES, send_next, 0)
 
     wait_count(ex_e.at[pl.ds(0, PEERS - 1)], red.at[5])
     fin_e[...] = (total(ex_e) * scale).astype(BF16)
@@ -591,13 +595,14 @@
     full = pltpu.VMEM((C, columns), F32)
     half = pltpu.VMEM((C, columns), BF16)
     big = pltpu.VMEM((FFN, columns), BF16)
-    cube = pltpu.VMEM((1024, C), F32)
+    cube = pltpu.VMEM((1024 + 8, C), F32)
     rows_e, rows_f = EARLY // ndp, LATE // ndp
     scratch = [
         pltpu.VMEM((1024, C), BF16), pltpu.VMEM((1, C), jnp.int32), pltpu.VMEM((3, C), F32),
         pltpu.VMEM((4, C, C), BF16), pltpu.VMEM((2, C, C), BF16),
         pltpu.VMEM((C, FFN), BF16), pltpu.VMEM((FFN, C), BF16),
         pltpu.SemaphoreType.DMA((7,)),
+        pltpu.VMEM((2, C, C), F32),
         pltpu.VMEM((C, C), F32),
         pltpu.VMEM((3, C, C), F32),
         pltpu.VMEM((4 * C, C), BF16),
@@ -608,7 +613,7 @@
         full, half, full, pltpu.VMEM((1, columns), F32), full, full, full, full,
         *([chunks] * 13),
         pltpu.VMEM((PEERS, 64, C), BF16),
-        pltpu.VMEM((PEERS * PACK, C), F32), pltpu.VMEM((PEERS * PACK, C), F32), cube, cube,
+        pltpu.VMEM((PEERS * PACK + 8, C), F32), pltpu.VMEM((PEERS * PACK + 8, C), F32), cube, cube,
         *([pltpu.VMEM((8, C, C), BF16)] * 3),
         half, big, half, half, big, full, pltpu.VMEM((5 * C, columns), BF16), half, half,
     ]

time: 82.8 us -> 80.9 us (0.977)
  Pallas kernels: 82 us -> 80.1 us
    pallas_call x1, Pallas kernels: 81 us -> 79.1 us  [local(): pl.pallas_call(functools.partial(kernel, ndp, scale), out_shape=outs, in_...]
where the time goes in v5:
time: 80.9 us; the launch traced here: 80.8 us
  Pallas kernels  80.1 us (99%)
    pallas_call x1, Pallas kernels, local(): pl.pallas_call(functools.partial(kernel, ndp, scale), out_shape=outs, in_...  79.1 us

profile of v5, /device:TPU:1, one launch (start us, length us, event | category | flops | bytes accessed | tf_op | source)
XLA Modules:
  0.0 80.8 jit_solution(4431815821044345301)
XLA Ops:
  0.6 79.1 %shard_map.135 = (bf16[1024,128]{1,0:T(8,128)(2,1)S(1)}, bf16[1024,128]{1,0:T(8,128)(2,1)S(1)}, bf16[512,128]{1,0:T(8,128)(2,1)S(1)}, bf16[256,128]{1,0:T(8,128)...) custom-call(bf16[1024,128]{1,0:T(8,128)(2,1)} %bitcast.6, ...), custom_call_target="tpu_custom_call" | custom-call | flops 1600000000 | bytes 3000000 | tf_op jit(solution)/shard_map/pallas_call | solution.py:647
  79.8 1.0 %shard_map.136 = (bf16[1024,128]{1,0:T(8,128)(2,1)}, bf16[1024,128]{1,0:T(8,128)(2,1)}, bf16[512,128]{1,0:T(8,128)(2,1)}, bf16[256,128]{1,0:T(8,128)(2,1)}, bf16...) custom-call(bf16[1024,128]{1,0:T(8,128)(2,1)S(1)} %get-tuple-element.21.refs_0_, ...), custom_call_target="tpu_custom_call" | custom-call | bytes 2000000 | tf_op jit(solution)/shard_map/pallas_call | solution.py:578
